TPU v7x, 256 devices: a whole 4x4x8 slice. The times are simulated.
256 devices in a mesh: dp: 2 (over core), frame: 16 (over x, y), mp: 8 (over z).
Axes of the slice: x: 4, y: 4, z: 8, core: 2. Of those that a mesh axis runs over, the one named last changes fastest.
Arguments:
- frames_in: bfloat16 [2, 16, 1024, 768], P('dp', 'frame'), may hold values from -6 to 6
- gain_space: float32 [768], replicated, may hold values from 0.1 to 1.9
- space_proj: bfloat16 [3, 768, 512], P(None, None, 'mp'), may hold values from -0.21875 to 0.21875
- space_out: bfloat16 [512, 768], replicated, may hold values from -0.25 to 0.25
- gain_time: float32 [768], replicated, may hold values from 0.1 to 1.9
- time_proj: bfloat16 [3, 768, 768], replicated, may hold values from -0.21875 to 0.21875
- time_out: bfloat16 [768, 768], replicated, may hold values from -0.21875 to 0.21875
- gain_mlp: float32 [768], replicated, may hold values from 0.1 to 1.9
- mlp_in: bfloat16 [3072, 768], P(('frame', 'mp')), may hold values from -0.21875 to 0.21875
- mlp_out: bfloat16 [3072, 768], P(('frame', 'mp')), may hold values from -0.109375 to 0.109375
- code_proj: bfloat16 [768, 32], replicated, may hold values from -0.21875 to 0.21875
- code_index: int32 [2, 16, 1024], P('dp', None, ('frame', 'mp')), may hold values from 0 to 1023, as said below
Outputs:
- block_out: bfloat16 [2, 16, 1024, 768], P('dp', None, ('frame', 'mp'))
- code_means: float32 [1024, 32], replicated
Inputs may be any that keep to these rules, and one draw needn't show every extreme that they name: `code_index`: at least 128 codes are named by no token; which ones is drawn from the seed.
All inputs are finite; a program needn't handle non-finite values.
Results may differ from a plain program's by a relative error of at most 0.017.
Values may be sent and summed in bfloat16 or wider, within the bound.
A program may use at most 64 MiB of HBM per device.

v0:
```python
import math

import jax
import jax.numpy as jnp
from jax import lax
from jax.sharding import PartitionSpec as P

HD = 64
CODES = 1024


def layer_norm(values, gain):
    center = jnp.mean(values, axis=-1, keepdims=True)
    spread = jnp.mean((values - center) ** 2, axis=-1, keepdims=True)
    return (values - center) * lax.rsqrt(spread + 1e-06) * gain


def attend_frame(queries, keys, values, factor):
    positions, heads_n, head_size = queries.shape
    block_rows = math.gcd(positions, 512)
    query_blocks = queries.reshape(positions // block_rows, block_rows, heads_n, head_size)

    def per_block(query_block):
        scores = (
            jnp.einsum("qhd,khd->hqk", query_block, keys, preferred_element_type=jnp.float32)
            * factor
        )
        weights = jax.nn.softmax(scores, axis=-1).astype(jnp.bfloat16)
        return jnp.einsum(
            "hqk,khd->qhd", weights, values, preferred_element_type=jnp.float32
        ).astype(jnp.bfloat16)

    return lax.map(per_block, query_blocks).reshape(positions, heads_n * head_size)


def attend_time(queries, keys, values, factor):
    frames_n = queries.shape[0]
    scores = (
        jnp.einsum("fnhd,gnhd->nhfg", queries, keys, preferred_element_type=jnp.float32) * factor
    )
    later = lax.broadcasted_iota(jnp.int32, (frames_n, frames_n), 0)
    earlier = lax.broadcasted_iota(jnp.int32, (frames_n, frames_n), 1)
    scores = jnp.where(earlier <= later, scores, -jnp.inf)
    weights = jax.nn.softmax(scores, axis=-1).astype(jnp.bfloat16)
    return jnp.einsum(
        "nhfg,gnhd->fnhd", weights, values, preferred_element_type=jnp.float32
    ).astype(jnp.bfloat16)


def unit_block(tokens, rows_in, rows_out):
    pre_act = lax.dot_general(
        tokens, rows_in, (((1,), (1,)), ((), ())), preferred_element_type=jnp.float32
    )
    hidden = jax.nn.gelu(pre_act, approximate=True).astype(jnp.bfloat16)
    return jnp.dot(hidden, rows_out, preferred_element_type=jnp.float32)


def shards(
    frames_in,
    gain_space,
    space_proj,
    space_out,
    gain_time,
    time_proj,
    time_out,
    gain_mlp,
    mlp_in,
    mlp_out,
    code_proj,
    code_index,
):
    factor = 1.0 / math.sqrt(HD)
    tokens = frames_in[0, 0]
    positions, features = tokens.shape
    normed = layer_norm(tokens.astype(jnp.float32), gain_space).astype(jnp.bfloat16)
    projected = jnp.einsum(
        "pd,sdc->spc", normed, space_proj, preferred_element_type=jnp.float32
    ).astype(jnp.bfloat16)
    heads_here = space_proj.shape[2] // HD
    projected = projected.reshape(3, positions, heads_here, HD)
    local_heads = attend_frame(projected[0], projected[1], projected[2], factor)
    col_width = features // lax.axis_size("mp")
    own_cols = lax.dynamic_slice_in_dim(tokens, lax.axis_index("mp") * col_width, col_width, 1)
    heads_all, token_rows = (
        lax.all_to_all(
            lax.all_to_all(local_heads[None], "frame", split_axis=1, concat_axis=0, tiled=True),
            "mp",
            split_axis=1,
            concat_axis=2,
            tiled=True,
        ),
        lax.all_to_all(
            lax.all_to_all(own_cols[None], "frame", split_axis=1, concat_axis=0, tiled=True),
            "mp",
            split_axis=1,
            concat_axis=2,
            tiled=True,
        ),
    )
    frames_n, pos_n, _ = token_rows.shape
    row_count = frames_n * pos_n
    after_space = token_rows.reshape(row_count, features).astype(jnp.float32) + jnp.dot(
        heads_all.reshape(row_count, -1), space_out, preferred_element_type=jnp.float32
    )
    time_in = layer_norm(after_space, gain_time).astype(jnp.bfloat16)
    time_qkv = jnp.einsum(
        "rd,sdc->src", time_in, time_proj, preferred_element_type=jnp.float32
    ).astype(jnp.bfloat16)
    time_qkv = time_qkv.reshape(3, frames_n, pos_n, features // HD, HD)
    time_heads = attend_time(time_qkv[0], time_qkv[1], time_qkv[2], factor).reshape(
        row_count, features
    )
    after_time = after_space + jnp.dot(time_heads, time_out, preferred_element_type=jnp.float32)
    mlp_act = layer_norm(after_time, gain_mlp).astype(jnp.bfloat16)
    after_mlp = after_time + unit_block(
        mlp_act,
        lax.all_gather(mlp_in, ("frame", "mp"), axis=0, tiled=True),
        lax.all_gather(mlp_out, ("frame", "mp"), axis=0, tiled=True),
    )
    outputs = after_mlp.astype(jnp.bfloat16)
    code_vec = jnp.dot(outputs, code_proj, preferred_element_type=jnp.float32)
    own_codes = code_index.reshape(row_count)
    onehot = (own_codes[:, None] == lax.broadcasted_iota(jnp.int32, (1, CODES), 1)).astype(
        jnp.float32
    )
    code_sums = lax.dot_general(
        onehot,
        code_vec,
        (((0,), (0,)), ((), ())),
        precision=lax.Precision.HIGHEST,
        preferred_element_type=jnp.float32,
    )
    code_counts = jnp.sum(onehot, axis=0)
    code_sums, code_counts = lax.psum((code_sums, code_counts), ("dp", "frame", "mp"))
    code_means = code_sums / jnp.maximum(code_counts, 1.0)[:, None]
    return (outputs.reshape(1, frames_n, pos_n, features), code_means)


def solution(mesh):
    placed = (
        P("dp", "frame", None, None),
        P(),
        P(None, None, "mp"),
        P(),
        P(),
        P(),
        P(),
        P(),
        P(("frame", "mp"), None),
        P(("frame", "mp"), None),
        P(),
        P("dp", None, ("frame", "mp")),
    )
    return jax.shard_map(
        shards,
        mesh=mesh,
        in_specs=placed,
        out_specs=(P("dp", None, ("frame", "mp"), None), P()),
        check_vma=False,
    )
```

profile of v0, /device:TPU:1, one launch (start us, length us, event | category | flops | bytes accessed | tf_op | source)
XLA Modules:
  0.0 506.0 jit_solution(569047426339073134)
XLA Ops:
  16.1 6.7 %while.10 = (s32[]{:T(128)}, bf16[2,512,1,64]{1,3,2,0:T(8,128)(2,1)}, bf16[2,512,1,64]{1,3,2,0:T(8,128)(2,1)}, bf16[1024,1,64]{0,2,1:T(8,128)(2,1)}, bf16[1024,1,64]{0,2,1:T(8,128)(2,1)}, /*index=5*/s32[]{:T(128)}) while((s32[]{:T(128)}, bf16[2,512,1,64]{1,3,2,0:T(8,128)(2,1)}, bf16[2,512,1,64]{1,3,2,0:T(8,128)(2,1)}, ...), condition=%wide.region_5.6_spmd, body=%wide.region_2.5_spmd.sunk | while | flops 138968064 | bytes 7220321 | solution.py:33
  24.6 2.6 reshape.124
  27.8 3.8 reduce.6
  33.5 7.7 %all-to-all-start.2 = ((bf16[16,2,2048]{2,1,0:T(2,128)(2,1)}), bf16[16,2,2048]{2,1,0:T(2,128)(2,1)}, u32[]{:S(2)}, u32[]{:S(2)}) async-start(bf16[16,2,2048]{2,1,0:T(2,128)(2,1)} %reshape.128), calls=%async_computation.2 | async-start | bytes 262144 | tf_op jit(solution)/shard_map/all_to_all | solution.py:86
  41.1 1.9 constant_dynamic-slice_fusion
  44.8 1.9 copy.76
  46.7 3.8 reduce.5
  50.6 2.1 reshape.126
  52.6 6.6 %all-to-all-start = ((bf16[16,2,3072]{2,1,0:T(2,128)(2,1)}), bf16[16,2,3072]{2,1,0:T(2,128)(2,1)}, u32[]{:S(2)}, u32[]{:S(2)}) async-start(bf16[16,2,3072]{2,1,0:T(2,128)(2,1)} %reshape.126), calls=%async_computation | async-start | bytes 393216 | tf_op jit(solution)/shard_map/all_to_all | solution.py:93
  66.3 8.2 %all-to-all-start.3 = ((bf16[8,2,4096]{2,1,0:T(2,128)(2,1)}), bf16[8,2,4096]{2,1,0:T(2,128)(2,1)}, u32[]{:S(2)}, u32[]{:S(2)}) async-start(bf16[8,2,4096]{2,1,0:T(2,128)(2,1)} %reshape.130), calls=%async_computation.3 | async-start | bytes 262144 | tf_op jit(solution)/shard_map/all_to_all | solution.py:85
  74.5 2.0 reshape.127
  78.4 4.4 all-to-all-done.3
  82.8 4.0 all-to-all-start.1
  87.2 78.6 %psum.15 = f32[1024]{0:T(1024)S(1)} all-reduce(f32[1024]{0:T(1024)S(1)} %convert_reduce_fusion.1), channel_id=1, replica_groups=mesh['dp'=2,'frame'=16,'mp'=8] {'dp','frame','mp'}, use_global_device_ids=true, to_apply=%region_14.15 | all-reduce | flops 1024 | bytes 8192 | tf_op jit(solution)/shard_map/psum | solution.py:134
  173.3 2.0 reshape.119
  178.6 2.1 squeeze.21
  180.7 2.1 squeeze.22
  182.8 2.1 squeeze.20
  188.4 2.9 fusion.34
  191.3 1.9 copy.91
  193.3 2.1 reshape.117
  198.6 49.2 %all-gather.5.cloned.1.call-done = bf16[3072,768]{1,0:T(8,128)(2,1)} async-done(((bf16[24,768]{1,0:T(8,128)(2,1)}), bf16[3072,768]{1,0:T(8,128)(2,1)}) %all-gather.5.cloned.1.call-update) | async-done | bytes 4718608 | tf_op jit(solution)/shard_map/all_gather | solution.py:118
  247.8 7.0 %fusion.35 = bf16[128,768]{1,0:T(8,128)(2,1)} fusion(f32[128,768]{1,0:T(8,128)} %copy-done.3, bf16[3072,768]{1,0:T(8,128)(2,1)} %all-gather.5.cloned.1.call-done, bf16[3072,768]{1,0:T(8,128)(2,1)} %all-gather.3.cloned.1.call-done, f32[768]{0:T(1024)S(1)} %copy-done.9, f32[128]{0:T(128)} %add_rsqrt_fusion.1, f32[128]{0:T(128)S(1)} %broadcast_multiply_fusion.1), kind=kOutput, calls=%fused_computation.47 | convolution fusion | flops 1212088320 | bytes 10031104 | tf_op jit(solution)/shard_map/dot_general | solution.py:55
  257.0 241.0 %all-reduce.2.cloned.1.call-done = f32[1024,32]{0,1:T(8,128)} async-done(((f32[1024,32]{0,1:T(8,128)}), f32[1024,32]{0,1:T(8,128)}) %all-reduce.2.cloned.1.call-update) | async-done | bytes 131088 | tf_op jit(solution)/shard_map/psum | solution.py:134
  (85 shorter events, 52.0 us)
Async XLA Ops:
  7.2 169.9 %copy-start = (bf16[3,768,768]{2,1,0:T(8,128)(2,1)S(1)}, bf16[3,768,768]{2,1,0:T(8,128)(2,1)}, u32[]{:S(2)}) copy-start(bf16[3,768,768]{2,1,0:T(8,128)(2,1)} %param.19) | copy-start | bytes 10616836
  7.2 4.0 copy-start.8
  7.2 191.4 %all-gather.3.cloned.1.call-start = ((), (), s32[]{:S(2)}) async-start(), calls=%async_computation.4 | async-start | bytes 4755456 | tf_op jit(solution)/shard_map/all_gather | solution.py:117
  7.9 239.9 %all-gather.5.cloned.1.call-start = ((), (), s32[]{:S(2)}) async-start(), calls=%async_computation.5 | async-start | bytes 4755456 | tf_op jit(solution)/shard_map/all_gather | solution.py:118
  8.7 1.9 copy-start.1
  8.7 2.5 copy-start.7
  16.1 2.0 copy-start.4
  19.5 2.0 copy-start.4
  33.5 19.2 %all-to-all-start.2 = ((bf16[16,2,2048]{2,1,0:T(2,128)(2,1)}), bf16[16,2,2048]{2,1,0:T(2,128)(2,1)}, u32[]{:S(2)}, u32[]{:S(2)}) async-start(bf16[16,2,2048]{2,1,0:T(2,128)(2,1)} %reshape.128), calls=%async_computation.2 | async-start | bytes 262144 | tf_op jit(solution)/shard_map/all_to_all | solution.py:86
  52.6 13.6 %all-to-all-start = ((bf16[16,2,3072]{2,1,0:T(2,128)(2,1)}), bf16[16,2,3072]{2,1,0:T(2,128)(2,1)}, u32[]{:S(2)}, u32[]{:S(2)}) async-start(bf16[16,2,3072]{2,1,0:T(2,128)(2,1)} %reshape.126), calls=%async_computation | async-start | bytes 393216 | tf_op jit(solution)/shard_map/all_to_all | solution.py:93
  61.2 25.8 %copy-start.5 = (s32[1,16,8]{1,2,0:T(8,128)S(1)}, s32[1,16,8]{1,2,0:T(8,128)}, u32[]{:S(2)}) copy-start(s32[1,16,8]{1,2,0:T(8,128)} %param.25) | copy-start | bytes 1540
  66.3 16.5 %all-to-all-start.3 = ((bf16[8,2,4096]{2,1,0:T(2,128)(2,1)}), bf16[8,2,4096]{2,1,0:T(2,128)(2,1)}, u32[]{:S(2)}, u32[]{:S(2)}) async-start(bf16[8,2,4096]{2,1,0:T(2,128)(2,1)} %reshape.130), calls=%async_computation.3 | async-start | bytes 262144 | tf_op jit(solution)/shard_map/all_to_all | solution.py:85
  82.8 88.5 %all-to-all-start.1 = ((bf16[16,64,96]{2,0,1:T(8,128)(2,1)}), bf16[16,64,96]{2,0,1:T(8,128)(2,1)}, u32[]{:S(2)}, u32[]{:S(2)}) async-start(bf16[16,64,96]{2,0,1:T(8,128)(2,1)} %copy.77), calls=%async_computation.1 | async-start | bytes 524288 | tf_op jit(solution)/shard_map/all_to_all | solution.py:92
  86.9 411.1 %all-reduce.2.cloned.1.call-start = ((), (), s32[]{:S(2)}) async-start(), calls=%async_computation.6 | async-start | bytes 262144 | tf_op jit(solution)/shard_map/psum | solution.py:134
  172.3 4.7 copy-start.6
  176.9 0.9 copy-start.2
  186.6 0.9 copy-start.10
  191.3 56.5 %copy-start.9 = (f32[768]{0:T(1024)S(1)}, f32[768]{0:T(1024)}, u32[]{:S(2)}) copy-start(f32[768]{0:T(1024)} %param.21) | copy-start | bytes 9220
  197.2 0.7 copy-start.3
Sparse Core Ops, SparseCore 0:
  11.7 118.2 all-gather.2
  133.7 114.0 all-gather.4
  257.1 240.8 all-reduce.1
where the time goes:
time: 508 us; the launch traced here: 506 us
  waiting for transfers between devices  297 us (58%)
  blocking collectives  78.6 us (15%)
  local copies, waits for them, and re-layouts  49.2 us (10%)
  starting transfers between devices  26.6 us (5%)
  matrix products  24.4 us (5%)
  other arithmetic  15.8 us (3%)
  between operations  14 us (3%)
    psum x1, waiting for transfers between devices, shards(): lax.psum((code_sums, code_counts), ('dp', 'frame', 'mp'))  241 us
    psum x1, blocking collectives, shards(): lax.psum((code_sums, code_counts), ('dp', 'frame', 'mp'))  78.6 us
    all_gather x1, waiting for transfers between devices, shards(): lax.all_gather(mlp_out, ('frame', 'mp'), axis=0, tiled=True)  49.2 us
    unnamed x31, local copies, waits for them, and re-layouts  17.7 us
  transfers between devices with their start and end apart: 7, of which 4 were waited for; matrix products, arithmetic and copies ran while one was open for 15% of the time, Pallas kernels for 0%

commit v1 on v0

v1 whole, which is shorter than its diff:
```python
import math

import jax
import jax.numpy as jnp
from jax import lax
from jax.experimental import pallas as pl
from jax.experimental.pallas import tpu as pltpu
from jax.sharding import PartitionSpec as P

F32 = jnp.float32
BF16 = jnp.bfloat16
MESH = pl.DeviceIdType.MESH

D = 768
HALF = D // 2
HD = 64
T_HEADS = 12
CODES = 1024
POS = 1024
FRAMES = 16
NX, NY, NZ = 4, 4, 8
SIZE = {"x": NX, "y": NY, "z": NZ}
ORDERS = (("x", "y", "z"), ("y", "z", "x"), ("z", "x", "y"))
UNITS = tuple(SIZE[order[0]] // 2 * 8 for order in ORDERS)


def layer_norm(values, gain):
    center = jnp.mean(values, axis=-1, keepdims=True)
    shifted = values - center
    spread = jnp.mean(shifted * shifted, axis=-1, keepdims=True)
    return shifted * lax.rsqrt(spread + 1e-06) * gain


def nt_dot(a, b):
    return lax.dot_general(a, b, (((1,), (1,)), ((), ())), preferred_element_type=F32)


def gelu(v):
    inner = math.sqrt(2.0 / math.pi) * (v + 0.044715 * (v * v * v))
    return 0.5 * v * (1.0 + jnp.tanh(inner))


def lanes(shape):
    return lax.broadcasted_iota(jnp.int32, shape, len(shape) - 1)


def block_kernel(
    frames_hbm, gs_ref, sproj_hbm, sout_hbm, gt_ref, tproj_hbm, tout_hbm, gm_ref,
    win_ref, wout_ref, cproj_ref, cidx_ref,
    out_ref, means_ref,
    fr, sp, so, tp, to, q_s, k_s, v_s,
    heads_send, heads_recv, rows_send, rows_recv,
    own_parts, first0, first1, first2, w0, w1, w2,
    act_send, act_recv, back_send, back_recv,
    sums_send, sums_recv, tot_all, mean_send, mean_recv,
    load_sem, heads_ss, heads_rs, rows_ss, rows_rs, first_ss, first_rs,
    ring_ss, ring_rs, pair_ss, pair_rs, red_ss, red_rs, tot_ss, tot_rs, fin_ss, fin_rs,
):
    c = lax.axis_index("dp")
    f = lax.axis_index("frame")
    m = lax.axis_index("mp")
    me = {"x": f // NY, "y": f % NY, "z": m}
    group = c * NZ + m

    def at(**moved):
        x = moved.get("x", me["x"])
        y = moved.get("y", me["y"])
        return (c, x * NY + y, moved.get("z", m))

    def frame_peer(k):
        return (c, (f + k) % FRAMES, m)

    def group_peer(k):
        other = (group + k) % 16
        return (other // NZ, f, other % NZ)

    barrier = pltpu.get_barrier_semaphore()

    @pl.loop(1, 16)
    def _(k):
        pl.semaphore_signal(barrier, inc=1, device_id=frame_peer(k), device_id_type=MESH)
        pl.semaphore_signal(barrier, inc=1, device_id=group_peer(k), device_id_type=MESH)

    loads = [pltpu.make_async_copy(sproj_hbm, sp, load_sem.at[0])]
    for i in range(4):
        rows = pl.ds(i * 256, 256)
        loads.append(pltpu.make_async_copy(frames_hbm.at[0, 0, rows], fr.at[rows], load_sem.at[1 + i]))
    loads.append(pltpu.make_async_copy(sout_hbm, so, load_sem.at[5]))
    loads.append(pltpu.make_async_copy(tproj_hbm, tp, load_sem.at[6]))
    loads.append(pltpu.make_async_copy(tout_hbm, to, load_sem.at[7]))
    for load in loads:
        load.start()

    win = win_ref[...].astype(F32)
    wout = wout_ref[...].astype(F32)
    for p in range(3):
        own_parts[p] = jnp.concatenate(
            [win[p * 8 : p * 8 + 8], wout[p * 8 : p * 8 + 8]], axis=0
        ).astype(BF16)
    firsts = (first0, first1, first2)
    gathered = (w0, w1, w2)
    waits = []

    def first_copy(p, k, slot):
        axis = ORDERS[p][0]
        return pltpu.make_async_remote_copy(
            src_ref=own_parts.at[p], dst_ref=firsts[p].at[slot],
            send_sem=first_ss.at[p, k], recv_sem=first_rs.at[p, slot],
            device_id=at(**{axis: (me[axis] + k) % SIZE[axis]}), device_id_type=MESH,
        )

    def first_send(p):
        axis = ORDERS[p][0]
        n = SIZE[axis]
        slot = me[axis] % (n // 2)

        @pl.when(me[axis] // (n // 2) == c)
        def _():
            firsts[p][slot] = own_parts[p]
            for k in range(1, n):
                first_copy(p, k, slot).start()

    def first_wait(p):
        axis = ORDERS[p][0]
        n = SIZE[axis]
        for slot in range(n // 2):
            @pl.when(c * (n // 2) + slot != me[axis])
            def _():
                first_copy(p, 1, slot).wait_recv()
        block = firsts[p][...].astype(F32).reshape(n // 2, 2, 8, D)
        at3, at2 = me[ORDERS[p][2]], me[ORDERS[p][1]]
        for side in range(2):
            gathered[p][at3, at2, side] = block[:, side].reshape(n // 2 * 8, D).astype(BF16)

    def first_done(p):
        axis = ORDERS[p][0]
        n = SIZE[axis]

        @pl.when(me[axis] // (n // 2) == c)
        def _():
            for k in range(1, n):
                first_copy(p, k, 0).wait_send()

    def ring_copy(p, phase, step, way):
        axis = ORDERS[p][phase]
        n = SIZE[axis]
        shift = (n - (step - 1)) if way == 0 else (step - 1)
        index = (me[axis] + shift) % n
        if phase == 1:
            block = gathered[p].at[me[ORDERS[p][2]], index]
            if step == n // 2:
                block = block.at[way]
        else:
            block = gathered[p].at[index]
            if step == n // 2:
                inner = SIZE[ORDERS[p][1]] // 2
                block = block.at[pl.ds(way * inner, inner)]
        to_index = (me[axis] + (1 if way == 0 else n - 1)) % n
        return pltpu.make_async_remote_copy(
            src_ref=block, dst_ref=block,
            send_sem=ring_ss.at[p, phase - 1, step - 1, way],
            recv_sem=ring_rs.at[p, phase - 1, step - 1, way],
            device_id=at(**{axis: to_index}), device_id_type=MESH,
        )

    plans = []
    for p in range(3):
        plan = [(1, s) for s in range(1, SIZE[ORDERS[p][1]] // 2 + 1)]
        plan += [(2, s) for s in range(1, SIZE[ORDERS[p][2]] // 2 + 1)]
        plans.append(plan)
    stage = [0, 0, 0]

    def advance(p):
        at_step = stage[p]
        stage[p] += 1
        if at_step == 0:
            first_send(p)
            return
        if at_step == 1:
            first_wait(p)
        else:
            for way in range(2):
                ring_copy(p, *plans[p][at_step - 2], way).wait_recv()
        if at_step <= len(plans[p]):
            for way in range(2):
                ring_copy(p, *plans[p][at_step - 1], way).start()

    def finish(p):
        while stage[p] < len(plans[p]) + 2:
            advance(p)

    pl.semaphore_wait(barrier, 30)
    for p in (2, 0, 1):
        advance(p)

    loads[0].wait()
    wqkv = jnp.concatenate(
        [sp[0], sp[1], sp[2], jnp.zeros((D, HD), BF16)], axis=1
    )
    gain_space = gs_ref[...].reshape(1, D)
    for i in range(4):
        loads[1 + i].wait()

    @pl.loop(0, 4)
    def _(i):
        rows = pl.ds(pl.multiple_of(i * 256, 256), 256)
        normed = layer_norm(fr[rows, :].astype(F32), gain_space).astype(BF16)
        both = jnp.dot(normed, wqkv, preferred_element_type=F32)
        qk = both[:, :128]
        low = lanes((256, 128)) < HD
        k_s[rows, :] = pltpu.roll(qk, HD, 1).astype(BF16)
        v = both[:, 128:]
        v_s[rows, :] = jnp.where(lanes((256, 128)) == HD, 1.0, v).astype(BF16)
        q = jnp.where(low, qk * (1.0 / math.sqrt(HD)), 0.0).reshape(4, NZ, 8, 128)
        for to_m in range(NZ):
            q_s[to_m, pl.ds(pl.multiple_of(i * 32, 32), 32), :] = (
                q[:, to_m].reshape(32, 128).astype(BF16)
            )

    for p in (0, 1, 2):
        advance(p)

    def heads_copy(shift):
        dest = (m + shift) % NZ
        return pltpu.make_async_remote_copy(
            src_ref=heads_send.at[dest], dst_ref=heads_recv.at[m],
            send_sem=heads_ss.at[shift], recv_sem=heads_rs.at[shift],
            device_id=(c, f, dest), device_id_type=MESH,
        )

    @pl.loop(0, NZ)
    def _(i):
        shift = 4 + ((i + 1) // 2) * (1 - 2 * (i % 2))
        dest = (m + shift) % NZ
        scores = nt_dot(q_s[dest], k_s[...])
        top = jnp.max(scores, axis=-1, keepdims=True)
        weights = jnp.exp(scores - top).astype(BF16)
        mixed = jnp.dot(weights, v_s[...], preferred_element_type=F32)
        mixed = mixed / mixed[:, HD : HD + 1]
        packed = jnp.where(lanes((64, 128)) < HD, mixed[:64], pltpu.roll(mixed[64:], HD, 1))
        heads_send[dest] = packed.astype(BF16)

        @pl.when(shift != 0)
        def _():
            heads_copy(shift).start()

        @pl.when(i == 2)
        def _():
            for p in range(3):
                advance(p)

        @pl.when(i == 5)
        def _():
            for p in range(3):
                advance(p)

    heads_recv[m] = heads_send[m]
    for k in range(1, NZ):
        heads_copy(k).wait_recv()
    advance(1)

    side = lanes((64, 128)) < HD
    upper, lower = [], []
    for i in range(NZ // 2):
        even = heads_recv[2 * i].astype(F32)
        odd = heads_recv[2 * i + 1].astype(F32)
        upper.append(jnp.where(side, even, pltpu.roll(odd, HD, 1)))
        lower.append(jnp.where(side, pltpu.roll(even, HD, 1), odd))
    heads_all = jnp.concatenate(
        [jnp.concatenate(upper, axis=1), jnp.concatenate(lower, axis=1)], axis=0
    ).astype(BF16)
    own = []
    for i in range(FRAMES):
        pair = fr[pl.ds(pl.multiple_of(i * 64 + (m // 2) * 16, 16), 16), :].astype(F32)
        own.append(jnp.where(m % 2 == 0, pair[:8], pair[8:]))
    loads[5].wait()
    after_space = jnp.concatenate(own, axis=0) + jnp.dot(
        heads_all, so[...], preferred_element_type=F32
    )
    split = after_space.reshape(FRAMES, 8, D)
    rows_send[...] = jnp.concatenate([split[:, :, :HALF], split[:, :, HALF:]], axis=1).astype(BF16)

    def rows_copy(k):
        dest = (f + k) % FRAMES
        return pltpu.make_async_remote_copy(
            src_ref=rows_send.at[dest], dst_ref=rows_recv.at[f],
            send_sem=rows_ss.at[k], recv_sem=rows_rs.at[k],
            device_id=(c, dest, m), device_id_type=MESH,
        )

    @pl.loop(1, FRAMES)
    def _(k):
        rows_copy(k).start()

    rows_recv[f] = rows_send[f]
    advance(1)
    advance(0)

    @pl.loop(1, FRAMES)
    def _(k):
        rows_copy(k).wait_recv()

    arrived = rows_recv[...].astype(F32)
    after_space = jnp.concatenate([arrived[:, :8], arrived[:, 8:]], axis=2).reshape(128, D)
    loads[6].wait()
    loads[7].wait()
    time_in = layer_norm(after_space, gt_ref[...].reshape(1, D)).astype(BF16)
    tq = jnp.dot(time_in, tp[0], preferred_element_type=F32) * (1.0 / math.sqrt(HD))
    tk = jnp.dot(time_in, tp[1], preferred_element_type=F32).astype(BF16)
    tv = jnp.dot(time_in, tp[2], preferred_element_type=F32).astype(BF16)
    row = lax.broadcasted_iota(jnp.int32, (128, 128), 0)
    col = lax.broadcasted_iota(jnp.int32, (128, 128), 1)
    seen = (row % 8 == col % 8) & (col // 8 <= row // 8)
    low = col < HD
    pieces = []
    for i in range(T_HEADS // 2):
        cut = slice(i * 128, i * 128 + 128)
        both = []
        for own_half in (low, jnp.logical_not(low)):
            scores = nt_dot(jnp.where(own_half, tq[:, cut], 0.0).astype(BF16), tk[:, cut])
            scores = jnp.where(seen, scores, -jnp.inf)
            weights = jnp.exp(scores - jnp.max(scores, axis=-1, keepdims=True))
            weights = weights / jnp.sum(weights, axis=-1, keepdims=True)
            both.append(jnp.dot(weights.astype(BF16), tv[:, cut], preferred_element_type=F32))
        pieces.append(jnp.where(low, both[0], both[1]).astype(BF16))
    advance(0)
    advance(2)
    time_heads = jnp.concatenate(pieces, axis=1)
    after_time = after_space + jnp.dot(time_heads, to[...], preferred_element_type=F32)
    act_send[...] = layer_norm(after_time, gm_ref[...].reshape(1, D)).astype(BF16)

    partner = (1 - c, f, m)
    act_copy = pltpu.make_async_remote_copy(
        src_ref=act_send, dst_ref=act_recv, send_sem=pair_ss.at[0], recv_sem=pair_rs.at[0],
        device_id=partner, device_id_type=MESH,
    )
    act_copy.start()
    for p in (2, 0, 1):
        finish(p)
    act_copy.wait_recv()
    act = jnp.concatenate([act_recv[...], act_send[...]], axis=0)
    partial = jnp.zeros((256, D), F32)
    for p in (2, 0, 1):
        n3 = gathered[p].shape[0]
        for lo in range(0, n3, n3 // 2):
            part = gathered[p][lo : lo + n3 // 2]
            hidden = gelu(nt_dot(act, part[:, :, 0].reshape(256, D))).astype(BF16)
            partial += jnp.dot(hidden, part[:, :, 1].reshape(256, D), preferred_element_type=F32)
    back_send[...] = partial[:128]
    back_copy = pltpu.make_async_remote_copy(
        src_ref=back_send, dst_ref=back_recv, send_sem=pair_ss.at[1], recv_sem=pair_rs.at[1],
        device_id=partner, device_id_type=MESH,
    )
    back_copy.start()
    after_time = after_time + partial[128:]
    codes = jnp.broadcast_to(cidx_ref[0][:, None, :], (FRAMES, 8, 8)).reshape(128, 8)
    diagonal = lax.broadcasted_iota(jnp.int32, (128, 8), 0) % 8 == lanes((128, 8))
    codes = jnp.sum(jnp.where(diagonal, codes, 0), axis=1, keepdims=True)
    onehot = (codes == lanes((128, CODES))).astype(F32).astype(BF16)
    code_proj = cproj_ref[...].astype(F32).T.astype(BF16)
    back_copy.wait_recv()
    outputs = (after_time + back_recv[...]).astype(BF16)
    out_ref[0] = outputs.astype(F32).reshape(FRAMES, 8, D).astype(BF16)

    vecs = nt_dot(code_proj, outputs)
    high = vecs.astype(BF16)
    rest = (vecs - high.astype(F32)).astype(BF16)
    ones = jnp.ones((8, 128), F32)
    zeros = jnp.zeros((8, 128), F32)
    high32, rest32 = high.astype(F32), rest.astype(F32)
    left = jnp.concatenate(
        [high32[:16], ones, high32[16:], ones, rest32[:16], zeros, rest32[16:], zeros], axis=0
    ).astype(BF16)
    sums = jnp.dot(left, onehot, preferred_element_type=F32)
    sums = sums[:48] + sums[48:]
    for to_c in range(2):
        for to_m in range(NZ):
            sums_send[to_c * NZ + to_m] = sums[
                to_c * 24 : to_c * 24 + 24, to_m * 128 : to_m * 128 + 128
            ]

    def group_copy(k, src, dst, send_sem, recv_sem):
        return pltpu.make_async_remote_copy(
            src_ref=src, dst_ref=dst, send_sem=send_sem.at[k], recv_sem=recv_sem.at[k],
            device_id=group_peer(k), device_id_type=MESH,
        )

    def sums_copy(k):
        return group_copy(k, sums_send.at[(group + k) % 16], sums_recv.at[k], red_ss, red_rs)

    def tot_copy(k):
        return pltpu.make_async_remote_copy(
            src_ref=tot_all.at[f], dst_ref=tot_all.at[f], send_sem=tot_ss.at[k],
            recv_sem=tot_rs.at[k], device_id=frame_peer(k), device_id_type=MESH,
        )

    def mean_copy(k):
        return group_copy(k, mean_send, mean_recv.at[group], fin_ss, fin_rs)

    @pl.loop(1, 16)
    def _(k):
        sums_copy(k).start()

    @pl.loop(1, 16)
    def _(k):
        sums_copy(k).wait_recv()

    total = sums_send[group]
    for k in range(1, 16):
        total += sums_recv[k]
    tot_all[f] = total

    @pl.loop(1, 16)
    def _(k):
        tot_copy(k).start()

    @pl.loop(1, 16)
    def _(k):
        tot_copy(k).wait_recv()

    total = tot_all[0]
    for k in range(1, 16):
        total += tot_all[k]
    means = total[:16] / jnp.maximum(total[16:17], 1.0)
    mean_send[...] = means
    mean_recv[group] = means

    @pl.loop(1, 16)
    def _(k):
        mean_copy(k).start()

    for p in range(3):
        first_done(p)
        for phase, step in plans[p]:
            for way in range(2):
                ring_copy(p, phase, step, way).wait_send()
    for k in range(1, NZ):
        heads_copy(k).wait_send()
    act_copy.wait_send()
    back_copy.wait_send()

    @pl.loop(1, 16)
    def _(k):
        rows_copy(k).wait_send()
        sums_copy(k).wait_send()
        tot_copy(k).wait_send()
        mean_copy(k).wait_send()
        mean_copy(k).wait_recv()

    for g in range(16):
        cut = slice(g % NZ * 128, g % NZ * 128 + 128)
        means_ref[g // NZ * 16 : g // NZ * 16 + 16, cut] = mean_recv[g]


def shards(*args):
    vmem = pl.BlockSpec(memory_space=pltpu.VMEM)
    hbm = pl.BlockSpec(memory_space=pltpu.HBM)
    dma = pltpu.SemaphoreType.DMA
    scratch = [
        pltpu.VMEM((POS, D), BF16),
        pltpu.VMEM((3, D, HD), BF16),
        pltpu.VMEM((512, D), BF16),
        pltpu.VMEM((3, D, D), BF16),
        pltpu.VMEM((D, D), BF16),
        pltpu.VMEM((NZ, 128, 128), BF16),
        pltpu.VMEM((POS, 128), BF16),
        pltpu.VMEM((POS, 128), BF16),
        pltpu.VMEM((NZ, 64, 128), BF16),
        pltpu.VMEM((NZ, 64, 128), BF16),
        pltpu.VMEM((FRAMES, 16, HALF), BF16),
        pltpu.VMEM((FRAMES, 16, HALF), BF16),
        pltpu.VMEM((3, 16, D), BF16),
    ]
    scratch += [pltpu.VMEM((SIZE[order[0]] // 2, 16, D), BF16) for order in ORDERS]
    scratch += [
        pltpu.VMEM((SIZE[order[2]], SIZE[order[1]], 2, units, D), BF16)
        for order, units in zip(ORDERS, UNITS)
    ]
    scratch += [
        pltpu.VMEM((128, D), BF16),
        pltpu.VMEM((128, D), BF16),
        pltpu.VMEM((128, D), F32),
        pltpu.VMEM((128, D), F32),
        pltpu.VMEM((16, 24, 128), F32),
        pltpu.VMEM((16, 24, 128), F32),
        pltpu.VMEM((FRAMES, 24, 128), F32),
        pltpu.VMEM((16, 128), F32),
        pltpu.VMEM((16, 16, 128), F32),
    ]
    scratch += [
        dma((8,)),
        dma((NZ,)), dma((NZ,)),
        dma((FRAMES,)), dma((FRAMES,)),
        dma((3, NZ)), dma((3, NZ)),
        dma((3, 2, 4, 2)), dma((3, 2, 4, 2)),
        dma((2,)), dma((2,)),
        dma((16,)), dma((16,)),
        dma((16,)), dma((16,)),
        dma((16,)), dma((16,)),
    ]
    block_out, means = pl.pallas_call(
        block_kernel,
        out_shape=(
            jax.ShapeDtypeStruct((1, FRAMES, 8, D), BF16),
            jax.ShapeDtypeStruct((32, CODES), F32),
        ),
        in_specs=[hbm, vmem, hbm, hbm, vmem, hbm, hbm, vmem, vmem, vmem, vmem, vmem],
        out_specs=(vmem, vmem),
        scratch_shapes=scratch,
        compiler_params=pltpu.CompilerParams(
            collective_id=0, has_side_effects=True, vmem_limit_bytes=48 * 1024 * 1024
        ),
    )(*args)
    return block_out, means.T


def solution(mesh):
    placed = (
        P("dp", "frame", None, None),
        P(),
        P(None, None, "mp"),
        P(),
        P(),
        P(),
        P(),
        P(),
        P(("frame", "mp"), None),
        P(("frame", "mp"), None),
        P(),
        P("dp", None, ("frame", "mp")),
    )
    return jax.shard_map(
        shards,
        mesh=mesh,
        in_specs=placed,
        out_specs=(P("dp", None, ("frame", "mp"), None), P()),
        check_vma=False,
    )
```

time: 508 us -> 90.9 us (0.18)
  waiting for transfers between devices: 297 us -> 0 us
  Pallas kernels: 0 us -> 79.1 us
  blocking collectives: 78.6 us -> 0 us
  local copies, waits for them, and re-layouts: 49.2 us -> 10.7 us
  starting transfers between devices: 26.6 us -> 0 us
  matrix products: 24.4 us -> 0 us
  other arithmetic: 15.8 us -> 0 us
  between operations: 14 us -> 0.68 us
    psum x1 -> x0, waiting for transfers between devices: 241 us -> none  [shards(): lax.psum((code_sums, code_counts), ('dp', 'frame', 'mp'))]
    pallas_call x0 -> x1, Pallas kernels: none -> 79.1 us  [shards(): pl.pallas_call(block_kernel, out_shape=(jax.ShapeDtypeStruct((1, FRAMES,...]
    psum x1 -> x0, blocking collectives: 78.6 us -> none  [shards(): lax.psum((code_sums, code_counts), ('dp', 'frame', 'mp'))]
    all_gather x2 -> x0, waiting for transfers between devices: 49.2 us -> none  [the longest x1 49.2 us: shards(): lax.all_gather(mlp_out, ('frame', 'mp'), axis=0, tiled=True)]
    all_to_all x4 -> x0, starting transfers between devices: 26.5 us -> none  [the longest x1 8.17 us: shards(): lax.all_to_all(lax.all_to_all(local_heads[None], 'frame', split_axis=1, c...]
    dot_general x12 -> x0, matrix products: 23.5 us -> none  [the longest x1 6.99 us: unit_block(): return jnp.dot(hidden, rows_out, preferred_element_type=jnp.float32)]
    unnamed x2 -> x0, other arithmetic: 7.69 us -> none
    unnamed x31 -> x21, local copies, waits for them, and re-layouts: 17.7 us -> 10.7 us
  transfers between devices with their start and end apart: 7 -> 0, of which waited for: 4 -> 0; matrix products, arithmetic and copies ran while one was open for 15% -> 0% of each run, Pallas kernels for 0% -> 0%
where the time goes in v1:
time: 90.9 us; the launch traced here: 90.4 us
  Pallas kernels  79.1 us (87%)
  local copies, waits for them, and re-layouts  10.7 us (12%)
    pallas_call x1, Pallas kernels, shards(): pl.pallas_call(block_kernel, out_shape=(jax.ShapeDtypeStruct((1, FRAMES,...  79.1 us
    unnamed x21, local copies, waits for them, and re-layouts  10.7 us

profile of v1, /device:TPU:1, one launch (start us, length us, event | category | flops | bytes accessed | tf_op | source)
XLA Modules:
  0.0 90.4 jit_solution(4640658106695956593)
XLA Ops:
  0.6 0.0 copy-start.2
  0.6 0.8 copy.16.cidx_ref
  1.5 1.0 %copy.15.cproj_ref = bf16[768,32]{1,0:T(8,128)(2,1)S(1)} copy(bf16[768,32]{0,1:T(8,128)(2,1)} %param.22) | data formatting | bytes 98304 | tf_op args[10]
  2.4 1.3 %copy.14.sproj_hbm = bf16[3,768,64]{2,1,0:T(8,128)(2,1)S(1)} copy(bf16[3,768,64]{1,2,0:T(8,128)(2,1)} %param.14) | data formatting | bytes 589824 | tf_op args[2]
  3.7 0.0 copy-done.2
  3.7 0.0 copy-start
  3.7 1.4 %copy-done = bf16[1,1,1024,768]{3,2,1,0:T(8,128)(2,1)S(1)} copy-done((bf16[1,1,1024,768]{3,2,1,0:T(8,128)(2,1)S(1)}, bf16[1,1,1024,768]{3,2,1,0:T(8,128)(2,1)}, u32[]{:S(2)}) %copy-start) | copy-done | bytes 1572888
  5.1 0.0 copy-start.1
  5.1 1.3 %copy-done.1 = bf16[768,768]{1,0:T(8,128)(2,1)S(1)} copy-done((bf16[768,768]{1,0:T(8,128)(2,1)S(1)}, bf16[768,768]{1,0:T(8,128)(2,1)}, u32[]{:S(2)}) %copy-start.1) | copy-done | bytes 1179672
  6.4 0.0 copy-start.3
  6.4 0.8 copy-done.3
  7.2 0.0 copy-start.4
  7.2 0.8 copy-done.4
  8.0 0.0 copy-start.5
  8.0 0.7 copy-done.5
  8.6 0.0 copy-start.6
  8.6 0.7 copy-done.6
  9.3 0.0 copy-start.7
  9.3 0.7 copy-done.7
  10.0 79.1 %shard_map.131 = (bf16[1,16,8,768]{3,2,1,0:T(8,128)(2,1)S(1)}, f32[32,1024]{1,0:T(8,128)S(1)}) custom-call(bf16[1,1,1024,768]{3,2,1,0:T(8,128)(2,1)S(1)} %copy-done, f32[768]{0:T(1024)S(1)} %copy-done.5, bf16[3,768,64]{2,1,0:T(8,128)(2,1)S(1)} %copy.14.sproj_hbm, bf16[512,768]{1,0:T(8,128)(2,1)S(1)} %copy-done.2, f32[768]{0:T(1024)S(1)} %copy-done.6, ...), custom_call_target="tpu_custom_call" | custom-call | tf_op jit(solution)/shard_map/pallas_call | solution.py:501
  89.1 0.7 copy.19
  89.8 0.7 copy.20
Async XLA Ops:
  0.6 3.1 %copy-start.2 = (bf16[512,768]{1,0:T(8,128)(2,1)S(1)}, bf16[512,768]{1,0:T(8,128)(2,1)}, u32[]{:S(2)}) copy-start(bf16[512,768]{1,0:T(8,128)(2,1)} %sout_hbm.1) | copy-start | bytes 2359300
  3.7 1.4 %copy-start = (bf16[1,1,1024,768]{3,2,1,0:T(8,128)(2,1)S(1)}, bf16[1,1,1024,768]{3,2,1,0:T(8,128)(2,1)}, u32[]{:S(2)}) copy-start(bf16[1,1,1024,768]{3,2,1,0:T(8,128)(2,1)} %frames_hbm.1) | copy-start | bytes 4718596
  5.1 1.3 %copy-start.1 = (bf16[768,768]{1,0:T(8,128)(2,1)S(1)}, bf16[768,768]{1,0:T(8,128)(2,1)}, u32[]{:S(2)}) copy-start(bf16[768,768]{1,0:T(8,128)(2,1)} %tout_hbm.1) | copy-start | bytes 3538948
  6.4 0.8 copy-start.3
  7.2 0.8 copy-start.4
  8.0 0.7 copy-start.5
  8.6 0.7 copy-start.6
  9.3 0.7 copy-start.7

commit v2 on v1

v2 whole, which is shorter than its diff:
```python
import math

import jax
import jax.numpy as jnp
from jax import lax
from jax.experimental import pallas as pl
from jax.experimental.pallas import tpu as pltpu
from jax.sharding import PartitionSpec as P

F32 = jnp.float32
BF16 = jnp.bfloat16
MESH = pl.DeviceIdType.MESH

D = 768
HALF = D // 2
HD = 64
T_HEADS = 12
CODES = 1024
POS = 1024
FRAMES = 16
NX, NY, NZ = 4, 4, 8
SIZE = {"x": NX, "y": NY, "z": NZ}
ORDERS = (("x", "y", "z"), ("z", "y", "x"), ("z", "x", "y"))
UNITS = tuple(SIZE[order[0]] // 2 * 8 for order in ORDERS)
EVENTS = (
    (0, 0), (1, 0), (0, 1, 1), (2, 0), (0, 1, 3), (0, 1, 2),
    (0, 2, 1, 0), (1, 2, 1, 0), (1, 1, 1),
    (0, 2, 1, 1), (2, 1, 1), (1, 1, 3), (1, 1, 2), (0, 2, 1, 3),
    (0, 2, 1, 2), (2, 1, 3), (2, 1, 2), (2, 2, 1, 0),
    (0, 2, 2, 0), (0, 2, 2, 1), (0, 2, 2, 3), (1, 2, 2, 0),
    (0, 2, 2, 2), (2, 2, 1, 1), (0, 2, 3, 0), (1, 2, 1, 1),
    (0, 2, 3, 1), (2, 2, 1, 3), (0, 2, 3, 3), (1, 2, 1, 3),
    (0, 2, 3, 2), (2, 2, 1, 2), (1, 2, 1, 2),
    (2, 2, 2, 0), (0, 2, 4, 0), (0, 2, 4, 1), (1, 2, 2, 1), (2, 2, 2, 1),
    (0, 2, 4, 3), (0, 2, 4, 2), (1, 2, 2, 3), (2, 2, 2, 3), (1, 2, 2, 2), (2, 2, 2, 2),
)


def layer_norm(values, gain):
    center = jnp.mean(values, axis=-1, keepdims=True)
    shifted = values - center
    spread = jnp.mean(shifted * shifted, axis=-1, keepdims=True)
    return shifted * lax.rsqrt(spread + 1e-06) * gain


def nt_dot(a, b):
    return lax.dot_general(a, b, (((1,), (1,)), ((), ())), preferred_element_type=F32)


def gelu(v):
    inner = math.sqrt(2.0 / math.pi) * (v + 0.044715 * (v * v * v))
    return 0.5 * v * (1.0 + jnp.tanh(inner))


def lanes(shape):
    return lax.broadcasted_iota(jnp.int32, shape, len(shape) - 1)


def block_kernel(
    frames_hbm, gs_hbm, sproj_hbm, sout_hbm, gt_hbm, tproj_hbm, tout_hbm, gm_hbm,
    win_hbm, wout_hbm, cproj_hbm, cidx_hbm,
    out_hbm, means_ref,
    fr, gs_ref, sp, so, gt_ref, tp, to, gm_ref, win_ref, wout_ref, cproj_ref, cidx_ref,
    q_s, k_s, v_s,
    heads_send, heads_recv, rows_send, rows_recv,
    own_parts, first0, first1, first2, w0, w1, w2,
    act_send, act_recv, back_send, back_recv,
    out_s, sums_send, sums_recv, red_send, red_recv, tot_all, mean_send, mean_recv,
    load_sem, heads_ss, heads_rs, rows_ss, rows_rs, first_ss, first_rs,
    second_ss, second_rs,    ring_ss, ring_rs, pair_ss, pair_rs, red_ss, red_rs, tot_ss, tot_rs, fin_ss, fin_rs,
):
    c = lax.axis_index("dp")
    f = lax.axis_index("frame")
    m = lax.axis_index("mp")
    me = {"x": f // NY, "y": f % NY, "z": m}
    group = c * NZ + m

    def at(**moved):
        x = moved.get("x", me["x"])
        y = moved.get("y", me["y"])
        return (c, x * NY + y, moved.get("z", m))

    def frame_peer(k):
        return (c, (f + k) % FRAMES, m)

    def group_peer(k):
        other = (group + k) % 16
        return (other // NZ, f, other % NZ)

    barrier = pltpu.get_barrier_semaphore()

    @pl.loop(1, 16)
    def _(k):
        pl.semaphore_signal(barrier, inc=1, device_id=frame_peer(k), device_id_type=MESH)
        pl.semaphore_signal(barrier, inc=1, device_id=group_peer(k), device_id_type=MESH)

    loads = {}
    for name, src, dst in (
        ("win", win_hbm, win_ref), ("wout", wout_hbm, wout_ref),
        ("gs", gs_hbm, gs_ref), ("sp", sproj_hbm, sp), ("fr", frames_hbm.at[0, 0], fr),
        ("so", sout_hbm, so), ("gt", gt_hbm, gt_ref), ("tp", tproj_hbm, tp),
        ("to", tout_hbm, to), ("gm", gm_hbm, gm_ref),
        ("cproj", cproj_hbm, cproj_ref), ("cidx", cidx_hbm, cidx_ref),
    ):
        loads[name] = pltpu.make_async_copy(src, dst, load_sem.at[len(loads)])
        loads[name].start()
    loads["win"].wait()
    loads["wout"].wait()

    win = win_ref[...].astype(F32)
    wout = wout_ref[...].astype(F32)
    for p in range(3):
        own_parts[p] = jnp.concatenate(
            [win[p * 8 : p * 8 + 8], wout[p * 8 : p * 8 + 8]], axis=0
        ).astype(BF16)
    firsts = (first0, first1, first2)
    gathered = (w0, w1, w2)

    def first_copy(p, k, slot):
        axis = ORDERS[p][0]
        return pltpu.make_async_remote_copy(
            src_ref=own_parts.at[p], dst_ref=firsts[p].at[slot],
            send_sem=first_ss.at[p, k], recv_sem=first_rs.at[p, slot],
            device_id=at(**{axis: (me[axis] + k) % SIZE[axis]}), device_id_type=MESH,
        )

    def first_send(p):
        axis = ORDERS[p][0]
        n = SIZE[axis]
        slot = me[axis] % (n // 2)

        @pl.when(me[axis] // (n // 2) == c)
        def _():
            firsts[p][slot] = own_parts[p]
            for k in range(1, n):
                first_copy(p, k, slot).start()

    def first_wait(p):
        axis = ORDERS[p][0]
        n = SIZE[axis]
        for slot in range(n // 2):
            @pl.when(c * (n // 2) + slot != me[axis])
            def _():
                first_copy(p, 1, slot).wait_recv()
        block = firsts[p][...].astype(F32).reshape(n // 2, 2, 8, D)
        at3, at2 = me[ORDERS[p][2]], me[ORDERS[p][1]]
        for side in range(2):
            gathered[p][at3, at2, side] = block[:, side].reshape(n // 2 * 8, D).astype(BF16)

    def first_done(p):
        axis = ORDERS[p][0]
        n = SIZE[axis]

        @pl.when(me[axis] // (n // 2) == c)
        def _():
            for k in range(1, n):
                first_copy(p, k, 0).wait_send()

    def second_copy(p, k):
        _, axis, last = ORDERS[p]
        block = gathered[p].at[me[last], me[axis]]
        return pltpu.make_async_remote_copy(
            src_ref=block, dst_ref=block,
            send_sem=second_ss.at[p, k], recv_sem=second_rs.at[p, k],
            device_id=at(**{axis: (me[axis] + k) % SIZE[axis]}), device_id_type=MESH,
        )

    def ring_copy(p, step, sub, way):
        _, inner, axis = ORDERS[p]
        n = SIZE[axis]
        shift = (n - (step - 1)) if way == 0 else (step - 1)
        block = gathered[p].at[
            (me[axis] + shift) % n, (me[inner] + SIZE[inner] - sub) % SIZE[inner]
        ]
        if step == n // 2:
            block = block.at[way]
        return pltpu.make_async_remote_copy(
            src_ref=block, dst_ref=block,
            send_sem=ring_ss.at[p, step - 1, sub, way],
            recv_sem=ring_rs.at[p, step - 1, sub, way],
            device_id=at(**{axis: (me[axis] + (1 if way == 0 else n - 1)) % n}),
            device_id_type=MESH,
        )

    def ring_send(p, step, sub):
        if step <= SIZE[ORDERS[p][2]] // 2:
            for way in range(2):
                ring_copy(p, step, sub, way).start()

    todo = list(EVENTS)

    def gather(count):
        for event in todo[:count]:
            p = event[0]
            if event[1] == 0:
                first_wait(p)
                for k in (1, 3, 2):
                    second_copy(p, k).start()
                ring_send(p, 1, 0)
            elif event[1] == 1:
                second_copy(p, event[2]).wait_recv()
                ring_send(p, 1, event[2])
            else:
                for way in range(2):
                    ring_copy(p, event[2], event[3], way).wait_recv()
                ring_send(p, event[2] + 1, event[3])
        del todo[:count]

    def gather_sent():
        for p in range(3):
            first_done(p)
            for k in range(1, 4):
                second_copy(p, k).wait_send()
            for step in range(1, SIZE[ORDERS[p][2]] // 2 + 1):
                for sub in range(4):
                    for way in range(2):
                        ring_copy(p, step, sub, way).wait_send()

    for name in ("gs", "sp", "fr"):
        loads[name].wait()
    wqkv = jnp.concatenate([sp[...].reshape(3 * HD, D), jnp.zeros((HD, D), BF16)], axis=0)
    gain_space = gs_ref[...].reshape(1, D)

    @pl.loop(0, 4)
    def _(i):
        rows = pl.ds(pl.multiple_of(i * 256, 256), 256)
        normed = layer_norm(fr[rows, :].astype(F32), gain_space).astype(BF16)
        both = nt_dot(normed, wqkv)
        qk = both[:, :128]
        low = lanes((256, 128)) < HD
        k_s[rows, :] = pltpu.roll(qk, HD, 1).astype(BF16)
        v = both[:, 128:]
        v_s[rows, :] = jnp.where(lanes((256, 128)) == HD, 1.0, v).astype(BF16)
        q = jnp.where(low, qk * (1.0 / math.sqrt(HD)), 0.0).reshape(4, NZ, 8, 128)
        for to_m in range(NZ):
            q_s[to_m, pl.ds(pl.multiple_of(i * 32, 32), 32), :] = (
                q[:, to_m].reshape(32, 128).astype(BF16)
            )

    pl.semaphore_wait(barrier, 30)
    for p in range(3):
        first_send(p)

    def heads_copy(shift):
        dest = (m + shift) % NZ
        return pltpu.make_async_remote_copy(
            src_ref=heads_send.at[dest], dst_ref=heads_recv.at[m],
            send_sem=heads_ss.at[shift], recv_sem=heads_rs.at[shift],
            device_id=(c, f, dest), device_id_type=MESH,
        )

    @pl.loop(0, NZ)
    def _(i):
        shift = 4 + ((i + 1) // 2) * (1 - 2 * (i % 2))
        dest = (m + shift) % NZ
        scores = nt_dot(q_s[dest], k_s[...])
        top = jnp.max(scores, axis=-1, keepdims=True)
        weights = jnp.exp(scores - top).astype(BF16)
        mixed = jnp.dot(weights, v_s[...], preferred_element_type=F32)
        mixed = mixed / mixed[:, HD : HD + 1]
        packed = jnp.where(lanes((64, 128)) < HD, mixed[:64], pltpu.roll(mixed[64:], HD, 1))
        heads_send[dest] = packed.astype(BF16)

        @pl.when(shift != 0)
        def _():
            heads_copy(shift).start()

        @pl.when(i == 5)
        def _():
            gather(1)

        @pl.when(i == 7)
        def _():
            gather(1)

    heads_recv[m] = heads_send[m]
    gather(4)
    for k in range(1, NZ):
        heads_copy(k).wait_recv()

    side = lanes((64, 128)) < HD
    upper, lower = [], []
    for i in range(NZ // 2):
        even = heads_recv[2 * i].astype(F32)
        odd = heads_recv[2 * i + 1].astype(F32)
        upper.append(jnp.where(side, even, pltpu.roll(odd, HD, 1)))
        lower.append(jnp.where(side, pltpu.roll(even, HD, 1), odd))
    heads_all = jnp.concatenate(
        [jnp.concatenate(upper, axis=1), jnp.concatenate(lower, axis=1)], axis=0
    ).astype(BF16)
    own = []
    for i in range(FRAMES):
        pair = fr[pl.ds(pl.multiple_of(i * 64 + (m // 2) * 16, 16), 16), :].astype(F32)
        own.append(jnp.where(m % 2 == 0, pair[:8], pair[8:]))
    loads["so"].wait()
    after_space = jnp.concatenate(own, axis=0) + jnp.dot(
        heads_all, so[...], preferred_element_type=F32
    )
    split = after_space.reshape(FRAMES, 8, D)
    rows_send[...] = jnp.concatenate([split[:, :, :HALF], split[:, :, HALF:]], axis=1).astype(BF16)

    def rows_copy(k):
        dest = (f + k) % FRAMES
        return pltpu.make_async_remote_copy(
            src_ref=rows_send.at[dest], dst_ref=rows_recv.at[f],
            send_sem=rows_ss.at[k], recv_sem=rows_rs.at[k],
            device_id=(c, dest, m), device_id_type=MESH,
        )

    @pl.loop(1, FRAMES)
    def _(k):
        rows_copy(k).start()

    rows_recv[f] = rows_send[f]
    gather(12)

    @pl.loop(1, FRAMES)
    def _(k):
        rows_copy(k).wait_recv()

    arrived = rows_recv[...].astype(F32)
    after_space = jnp.concatenate([arrived[:, :8], arrived[:, 8:]], axis=2).reshape(128, D)
    for name in ("gt", "tp", "to", "gm", "cproj", "cidx"):
        loads[name].wait()
    time_in = layer_norm(after_space, gt_ref[...].reshape(1, D)).astype(BF16)
    tq = jnp.dot(time_in, tp[0], preferred_element_type=F32) * (1.0 / math.sqrt(HD))
    tk = jnp.dot(time_in, tp[1], preferred_element_type=F32).astype(BF16)
    tv = jnp.dot(time_in, tp[2], preferred_element_type=F32).astype(BF16)
    gather(1)
    row = lax.broadcasted_iota(jnp.int32, (128, 128), 0)
    col = lax.broadcasted_iota(jnp.int32, (128, 128), 1)
    seen = (row % 8 == col % 8) & (col // 8 <= row // 8)
    low = col < HD
    pieces = []
    for i in range(T_HEADS // 2):
        cut = slice(i * 128, i * 128 + 128)
        both = []
        for own_half in (low, jnp.logical_not(low)):
            scores = nt_dot(jnp.where(own_half, tq[:, cut], 0.0).astype(BF16), tk[:, cut])
            scores = jnp.where(seen, scores, -jnp.inf)
            weights = jnp.exp(scores - jnp.max(scores, axis=-1, keepdims=True))
            weights = weights / jnp.sum(weights, axis=-1, keepdims=True)
            both.append(jnp.dot(weights.astype(BF16), tv[:, cut], preferred_element_type=F32))
        pieces.append(jnp.where(low, both[0], both[1]).astype(BF16))
        gather((1, 2, 0, 2, 0, 2)[i])
    time_heads = jnp.concatenate(pieces, axis=1)
    after_time = after_space + jnp.dot(time_heads, to[...], preferred_element_type=F32)
    gather(2)
    act_send[...] = layer_norm(after_time, gm_ref[...].reshape(1, D)).astype(BF16)

    partner = (1 - c, f, m)
    act_copy = pltpu.make_async_remote_copy(
        src_ref=act_send, dst_ref=act_recv, send_sem=pair_ss.at[0], recv_sem=pair_rs.at[0],
        device_id=partner, device_id_type=MESH,
    )
    act_copy.start()
    gather(7)
    act_copy.wait_recv()
    act = jnp.concatenate([act_recv[...], act_send[...]], axis=0)
    partial = jnp.zeros((256, D), F32)
    for late in range(2):
        for p in (1, 0, 2):
            at3 = me[ORDERS[p][2]]
            if p == 0:
                steps = (6, 3, 5, 4) if late else (0, 1, 7, 2)
            else:
                steps = (3, 2) if late else (0, 1)
            part = [gathered[p][(at3 + step) % SIZE[ORDERS[p][2]]] for step in steps]
            w_in = jnp.concatenate([block[:, 0].reshape(-1, D) for block in part], axis=0)
            w_out = jnp.concatenate([block[:, 1].reshape(-1, D) for block in part], axis=0)
            hidden = gelu(nt_dot(act, w_in)).astype(BF16)
            partial += jnp.dot(hidden, w_out, preferred_element_type=F32)
        gather(len(todo))
    back_send[...] = partial[:128]
    back_copy = pltpu.make_async_remote_copy(
        src_ref=back_send, dst_ref=back_recv, send_sem=pair_ss.at[1], recv_sem=pair_rs.at[1],
        device_id=partner, device_id_type=MESH,
    )
    back_copy.start()
    after_time = after_time + partial[128:]
    codes = jnp.broadcast_to(cidx_ref[...], (FRAMES, 8, FRAMES)).reshape(128, FRAMES)
    diagonal = lax.broadcasted_iota(jnp.int32, (128, FRAMES), 0) // 8 == lanes((128, FRAMES))
    codes = jnp.sum(jnp.where(diagonal, codes, 0), axis=1, keepdims=True)
    onehot = (codes == lanes((128, CODES))).astype(F32).astype(BF16)
    back_copy.wait_recv()
    outputs = (after_time + back_recv[...]).astype(BF16)
    out_s[0] = outputs.astype(F32).reshape(FRAMES, 8, D).astype(BF16)
    out_copy = pltpu.make_async_copy(out_s, out_hbm, load_sem.at[0])
    out_copy.start()

    vecs = nt_dot(cproj_ref[...], outputs)
    high = vecs.astype(BF16)
    rest = (vecs - high.astype(F32)).astype(BF16)
    left = jnp.concatenate([high, rest, jnp.ones((16, 128), BF16)], axis=0)
    sums = jnp.dot(left, onehot, preferred_element_type=F32)
    counts = sums[64:72]
    sums = sums[:32] + sums[32:64]
    for to_c in range(2):
        for to_m in range(NZ):
            cut = slice(to_m * 128, to_m * 128 + 128)
            sums_send[to_c, to_m] = jnp.concatenate(
                [sums[to_c * 16 : to_c * 16 + 16, cut], counts[:, cut]], axis=0
            )
    sums_copy = pltpu.make_async_remote_copy(
        src_ref=sums_send.at[1 - c], dst_ref=sums_recv, send_sem=pair_ss.at[2],
        recv_sem=pair_rs.at[2], device_id=partner, device_id_type=MESH,
    )
    sums_copy.start()

    def coded(values):
        many = values[..., 16:24, :]
        upper = jnp.floor(many * (1.0 / 256.0))
        return jnp.concatenate(
            [values[..., :16, :], many - 256.0 * upper, upper], axis=-2
        ).astype(BF16)

    def decoded(values):
        values = values.astype(F32)
        return jnp.concatenate(
            [values[..., :16, :], values[..., 16:24, :] + 256.0 * values[..., 24:, :]], axis=-2
        )

    def red_copy(k):
        dest = (m + k) % NZ
        return pltpu.make_async_remote_copy(
            src_ref=red_send.at[dest], dst_ref=red_recv.at[k], send_sem=red_ss.at[k],
            recv_sem=red_rs.at[k], device_id=(c, f, dest), device_id_type=MESH,
        )

    def tot_copy(k):
        return pltpu.make_async_remote_copy(
            src_ref=tot_all.at[f], dst_ref=tot_all.at[f], send_sem=tot_ss.at[k],
            recv_sem=tot_rs.at[k], device_id=frame_peer(k), device_id_type=MESH,
        )

    def mean_copy(k):
        return pltpu.make_async_remote_copy(
            src_ref=mean_send, dst_ref=mean_recv.at[group], send_sem=fin_ss.at[k],
            recv_sem=fin_rs.at[k], device_id=group_peer(k), device_id_type=MESH,
        )

    sums_copy.wait_recv()
    red_send[...] = coded(sums_send[c] + sums_recv[...])
    for k in (4, 3, 5, 2, 6, 1, 7):
        red_copy(k).start()
    gather_sent()
    red_recv[0] = red_send[m]
    for k in range(1, NZ):
        red_copy(k).wait_recv()
    tot_all[f] = coded(jnp.sum(decoded(red_recv[...]), axis=0))

    @pl.loop(1, 16)
    def _(k):
        tot_copy(k).start()

    for k in range(1, NZ):
        heads_copy(k).wait_send()
        red_copy(k).wait_send()
    act_copy.wait_send()
    back_copy.wait_send()
    sums_copy.wait_send()

    @pl.loop(1, 16)
    def _(k):
        rows_copy(k).wait_send()

    @pl.loop(1, 16)
    def _(k):
        tot_copy(k).wait_recv()

    total = jnp.sum(decoded(tot_all[...]), axis=0)
    means = (total[:16] / jnp.maximum(total[16:17], 1.0)).astype(BF16)
    mean_send[...] = means
    mean_recv[group] = means

    @pl.loop(1, 16)
    def _(k):
        mean_copy(k).start()

    @pl.loop(1, 16)
    def _(k):
        tot_copy(k).wait_send()
        mean_copy(k).wait_send()

    out_copy.wait()

    @pl.loop(1, 16)
    def _(k):
        mean_copy(k).wait_recv()

    for g in range(16):
        cut = slice(g % NZ * 128, g % NZ * 128 + 128)
        means_ref[g // NZ * 16 : g // NZ * 16 + 16, cut] = mean_recv[g].astype(F32)


def shards(*args):
    args = list(args)
    args[2] = args[2].swapaxes(1, 2)
    args[10] = args[10].T
    args[11] = args[11].swapaxes(1, 2)
    vmem = pl.BlockSpec(memory_space=pltpu.VMEM)
    hbm = pl.BlockSpec(memory_space=pltpu.HBM)
    dma = pltpu.SemaphoreType.DMA
    scratch = [
        pltpu.VMEM((POS, D), BF16),
        pltpu.VMEM((D,), F32),
        pltpu.VMEM((3, HD, D), BF16),
        pltpu.VMEM((512, D), BF16),
        pltpu.VMEM((D,), F32),
        pltpu.VMEM((3, D, D), BF16),
        pltpu.VMEM((D, D), BF16),
        pltpu.VMEM((D,), F32),
        pltpu.VMEM((24, D), BF16),
        pltpu.VMEM((24, D), BF16),
        pltpu.VMEM((32, D), BF16),
        pltpu.VMEM((1, 8, FRAMES), jnp.int32),
        pltpu.VMEM((NZ, 128, 128), BF16),
        pltpu.VMEM((POS, 128), BF16),
        pltpu.VMEM((POS, 128), BF16),
        pltpu.VMEM((NZ, 64, 128), BF16),
        pltpu.VMEM((NZ, 64, 128), BF16),
        pltpu.VMEM((FRAMES, 16, HALF), BF16),
        pltpu.VMEM((FRAMES, 16, HALF), BF16),
        pltpu.VMEM((3, 16, D), BF16),
    ]
    scratch += [pltpu.VMEM((SIZE[order[0]] // 2, 16, D), BF16) for order in ORDERS]
    scratch += [
        pltpu.VMEM((SIZE[order[2]], SIZE[order[1]], 2, units, D), BF16)
        for order, units in zip(ORDERS, UNITS)
    ]
    scratch += [
        pltpu.VMEM((128, D), BF16),
        pltpu.VMEM((128, D), BF16),
        pltpu.VMEM((128, D), F32),
        pltpu.VMEM((128, D), F32),
        pltpu.VMEM((1, FRAMES, 8, D), BF16),
        pltpu.VMEM((2, NZ, 24, 128), F32),
        pltpu.VMEM((NZ, 24, 128), F32),
        pltpu.VMEM((NZ, 32, 128), BF16),
        pltpu.VMEM((NZ, 32, 128), BF16),
        pltpu.VMEM((FRAMES, 32, 128), BF16),
        pltpu.VMEM((16, 128), BF16),
        pltpu.VMEM((16, 16, 128), BF16),
    ]
    scratch += [
        dma((12,)),
        dma((NZ,)), dma((NZ,)),
        dma((FRAMES,)), dma((FRAMES,)),
        dma((3, NZ)), dma((3, NZ)),
        dma((3, 4)), dma((3, 4)),
        dma((3, 4, 4, 2)), dma((3, 4, 4, 2)),
        dma((3,)), dma((3,)),
        dma((NZ,)), dma((NZ,)),
        dma((16,)), dma((16,)),
        dma((16,)), dma((16,)),
    ]
    block_out, means = pl.pallas_call(
        block_kernel,
        out_shape=(
            jax.ShapeDtypeStruct((1, FRAMES, 8, D), BF16),
            jax.ShapeDtypeStruct((32, CODES), F32),
        ),
        in_specs=[hbm] * 12,
        out_specs=(hbm, vmem),
        scratch_shapes=scratch,
        compiler_params=pltpu.CompilerParams(
            collective_id=0, has_side_effects=True, vmem_limit_bytes=60 * 1024 * 1024
        ),
    )(*args)
    return block_out, means.T


def solution(mesh):
    placed = (
        P("dp", "frame", None, None),
        P(),
        P(None, None, "mp"),
        P(),
        P(),
        P(),
        P(),
        P(),
        P(("frame", "mp"), None),
        P(("frame", "mp"), None),
        P(),
        P("dp", None, ("frame", "mp")),
    )
    return jax.shard_map(
        shards,
        mesh=mesh,
        in_specs=placed,
        out_specs=(P("dp", None, ("frame", "mp"), None), P()),
        check_vma=False,
    )
```

time: 90.9 us -> 69 us (0.76)
  Pallas kernels: 79.1 us -> 65.1 us
  local copies, waits for them, and re-layouts: 10.7 us -> 3.18 us
    pallas_call x1, Pallas kernels: 79.1 us -> 65.1 us  [shards(): pl.pallas_call(block_kernel, out_shape=(jax.ShapeDtypeStruct((1, FRAMES,...]
    unnamed x21 -> x2, local copies, waits for them, and re-layouts: 10.7 us -> 3.18 us
where the time goes in v2:
time: 69 us; the launch traced here: 68.9 us
  Pallas kernels  65.1 us (94%)
  local copies, waits for them, and re-layouts  3.18 us (5%)
    pallas_call x1, Pallas kernels, shards(): pl.pallas_call(block_kernel, out_shape=(jax.ShapeDtypeStruct((1, FRAMES,...  65.1 us
    unnamed x2, local copies, waits for them, and re-layouts  3.18 us

profile of v2, /device:TPU:1, one launch (start us, length us, event | category | flops | bytes accessed | tf_op | source)
XLA Modules:
  0.0 68.9 jit_solution(7465096739512836500)
XLA Ops:
  0.6 65.1 %shard_map.131 = (bf16[1,16,8,768]{3,2,1,0:T(8,128)(2,1)}, f32[32,1024]{1,0:T(8,128)}) custom-call(bf16[1,1,1024,768]{3,2,1,0:T(8,128)(2,1)} %frames_hbm.1, f32[768]{0:T(1024)} %gs_hbm.1, bf16[3,64,768]{2,1,0:T(8,128)(2,1)} %bitcast.4, bf16[512,768]{1,0:T(8,128)(2,1)} %sout_hbm.1, f32[768]{0:T(1024)} %gt_hbm.1, bf16[3,768,768]{2,1,0:T(8,128)(2,1)} %tproj_hbm.1, ...), custom_call_target="tpu_custom_call" | custom-call | tf_op jit(solution)/shard_map/pallas_call | solution.py:557
  65.7 1.6 %copy.16 = bf16[1,16,8,768]{3,2,1,0:T(8,128)(2,1)} copy(bf16[1,16,8,768]{3,2,1,0:T(8,128)(2,1)} %get-tuple-element.8) | data formatting | bytes 393216
  67.3 1.6 %copy.17 = f32[1024,32]{0,1:T(8,128)} copy(f32[1024,32]{0,1:T(8,128)} %bitcast.5) | data formatting | bytes 262144

commit v3 on v2

--- a/solution.py
+++ b/solution.py
@@ -32,8 +32,18 @@
     (0, 2, 3, 1), (2, 2, 1, 3), (0, 2, 3, 3), (1, 2, 1, 3),
     (0, 2, 3, 2), (2, 2, 1, 2), (1, 2, 1, 2),
     (2, 2, 2, 0), (0, 2, 4, 0), (0, 2, 4, 1), (1, 2, 2, 1), (2, 2, 2, 1),
-    (0, 2, 4, 3), (0, 2, 4, 2), (1, 2, 2, 3), (2, 2, 2, 3), (1, 2, 2, 2), (2, 2, 2, 2),
+    (0, 2, 4, 3), (1, 2, 2, 3), (0, 2, 4, 2), (2, 2, 2, 3), (1, 2, 2, 2), (2, 2, 2, 2),
 )
+GATHER_AT = (0, 0, 0, 1, 6, 21, 22, 26, 28, 29)
+MLP_GROUPS = (
+    (29, ((0, (0, 1, 7, 2)),)),
+    (32, ((2, (0, 1)),)),
+    (33, ((1, (0, 1)),)),
+    (33, ((0, (6, 3, 5)), (1, (3,)))),
+    (41, ((2, (3,)), (0, (4,)))),
+    (44, ((1, (2,)), (2, (2,)))),
+)
+SOURCES = {"x": ((0, 1), (2, 3)), "z": ((0, 1), (2, 7), (6, 3), (4, 5))}
 
 
 def layer_norm(values, gain):
@@ -64,10 +74,12 @@
     q_s, k_s, v_s,
     heads_send, heads_recv, rows_send, rows_recv,
     own_parts, first0, first1, first2, w0, w1, w2,
+    cidx_recv, hot, count_send, count_recv, count_all,
     act_send, act_recv, back_send, back_recv,
-    out_s, sums_send, sums_recv, red_send, red_recv, tot_all, mean_send, mean_recv,
+    out_s, red_send, red_recv, tot_all, mean_send, mean_recv,
     load_sem, heads_ss, heads_rs, rows_ss, rows_rs, first_ss, first_rs,
     second_ss, second_rs,    ring_ss, ring_rs, pair_ss, pair_rs, red_ss, red_rs, tot_ss, tot_rs, fin_ss, fin_rs,
+    count_ss, count_rs, all_count_ss, all_count_rs,
 ):
     c = lax.axis_index("dp")
     f = lax.axis_index("frame")
@@ -116,45 +128,49 @@
     firsts = (first0, first1, first2)
     gathered = (w0, w1, w2)
 
-    def first_copy(p, k, slot):
+    def first_copy(p, slot):
         axis = ORDERS[p][0]
+        zero, one = SOURCES[axis][slot]
+        back = SIZE[axis] - zero - c * (one - zero)
         return pltpu.make_async_remote_copy(
             src_ref=own_parts.at[p], dst_ref=firsts[p].at[slot],
-            send_sem=first_ss.at[p, k], recv_sem=first_rs.at[p, slot],
-            device_id=at(**{axis: (me[axis] + k) % SIZE[axis]}), device_id_type=MESH,
+            send_sem=first_ss.at[p, slot], recv_sem=first_rs.at[p, slot],
+            device_id=at(**{axis: (me[axis] + back) % SIZE[axis]}), device_id_type=MESH,
         )
 
     def first_send(p):
-        axis = ORDERS[p][0]
-        n = SIZE[axis]
-        slot = me[axis] % (n // 2)
-
-        @pl.when(me[axis] // (n // 2) == c)
+        for slot in range(1, len(SOURCES[ORDERS[p][0]])):
+            first_copy(p, slot).start()
+
+        @pl.when(c == 1)
         def _():
-            firsts[p][slot] = own_parts[p]
-            for k in range(1, n):
-                first_copy(p, k, slot).start()
+            first_copy(p, 0).start()
+
+        @pl.when(c == 0)
+        def _():
+            firsts[p][0] = own_parts[p]
 
     def first_wait(p):
-        axis = ORDERS[p][0]
-        n = SIZE[axis]
-        for slot in range(n // 2):
-            @pl.when(c * (n // 2) + slot != me[axis])
-            def _():
-                first_copy(p, 1, slot).wait_recv()
+        n = SIZE[ORDERS[p][0]]
+        for slot in range(1, n // 2):
+            first_copy(p, slot).wait_recv()
+
+        @pl.when(c == 1)
+        def _():
+            first_copy(p, 0).wait_recv()
+
         block = firsts[p][...].astype(F32).reshape(n // 2, 2, 8, D)
         at3, at2 = me[ORDERS[p][2]], me[ORDERS[p][1]]
         for side in range(2):
             gathered[p][at3, at2, side] = block[:, side].reshape(n // 2 * 8, D).astype(BF16)
 
     def first_done(p):
-        axis = ORDERS[p][0]
-        n = SIZE[axis]
-
-        @pl.when(me[axis] // (n // 2) == c)
+        for slot in range(1, len(SOURCES[ORDERS[p][0]])):
+            first_copy(p, slot).wait_send()
+
+        @pl.when(c == 1)
         def _():
-            for k in range(1, n):
-                first_copy(p, k, 0).wait_send()
+            first_copy(p, 0).wait_send()
 
     def second_copy(p, k):
         _, axis, last = ORDERS[p]
@@ -189,7 +205,8 @@
 
     todo = list(EVENTS)
 
-    def gather(count):
+    def gather(until):
+        count = until - len(EVENTS) + len(todo)
         for event in todo[:count]:
             p = event[0]
             if event[1] == 0:
@@ -230,16 +247,28 @@
         low = lanes((256, 128)) < HD
         k_s[rows, :] = pltpu.roll(qk, HD, 1).astype(BF16)
         v = both[:, 128:]
-        v_s[rows, :] = jnp.where(lanes((256, 128)) == HD, 1.0, v).astype(BF16)
+        v_s[rows, :] = jnp.where(low, v, 1.0).astype(BF16)
         q = jnp.where(low, qk * (1.0 / math.sqrt(HD)), 0.0).reshape(4, NZ, 8, 128)
         for to_m in range(NZ):
             q_s[to_m, pl.ds(pl.multiple_of(i * 32, 32), 32), :] = (
                 q[:, to_m].reshape(32, 128).astype(BF16)
             )
 
+    partner = (1 - c, f, m)
+
+    def pair_copy(i, src, dst):
+        return pltpu.make_async_remote_copy(
+            src_ref=src, dst_ref=dst, send_sem=pair_ss.at[i], recv_sem=pair_rs.at[i],
+            device_id=partner, device_id_type=MESH,
+        )
+
+    for name in ("gt", "tp", "to", "gm", "cproj", "cidx"):
+        loads[name].wait()
     pl.semaphore_wait(barrier, 30)
     for p in range(3):
         first_send(p)
+    codes_copy = pair_copy(2, cidx_ref, cidx_recv)
+    codes_copy.start()
 
     def heads_copy(shift):
         dest = (m + shift) % NZ
@@ -249,32 +278,55 @@
             device_id=(c, f, dest), device_id_type=MESH,
         )
 
-    @pl.loop(0, NZ)
-    def _(i):
-        shift = 4 + ((i + 1) // 2) * (1 - 2 * (i % 2))
-        dest = (m + shift) % NZ
-        scores = nt_dot(q_s[dest], k_s[...])
-        top = jnp.max(scores, axis=-1, keepdims=True)
-        weights = jnp.exp(scores - top).astype(BF16)
+    half = lanes((64, 128)) < HD
+    for i, shifts in enumerate(((4, 3), (5, 2), (6, 1), (7, 0))):
+        queries = jnp.concatenate([q_s[(m + shift) % NZ] for shift in shifts], axis=0)
+        scores = nt_dot(queries, k_s[...])
+        weights = jnp.exp(scores - jnp.max(scores, axis=-1, keepdims=True)).astype(BF16)
         mixed = jnp.dot(weights, v_s[...], preferred_element_type=F32)
-        mixed = mixed / mixed[:, HD : HD + 1]
-        packed = jnp.where(lanes((64, 128)) < HD, mixed[:64], pltpu.roll(mixed[64:], HD, 1))
-        heads_send[dest] = packed.astype(BF16)
-
-        @pl.when(shift != 0)
-        def _():
-            heads_copy(shift).start()
-
-        @pl.when(i == 5)
-        def _():
-            gather(1)
-
-        @pl.when(i == 7)
-        def _():
-            gather(1)
+        turned = pltpu.roll(mixed, HD, 1)
+        for j, shift in enumerate(shifts):
+            top, bottom = slice(j * 128, j * 128 + 64), slice(j * 128 + 64, j * 128 + 128)
+            heads_send[(m + shift) % NZ] = (
+                jnp.where(half, mixed[top], turned[bottom])
+                / jnp.where(half, turned[top], mixed[bottom])
+            ).astype(BF16)
+        for shift in shifts:
+            if shift:
+                heads_copy(shift).start()
+        gather(GATHER_AT[i])
 
     heads_recv[m] = heads_send[m]
-    gather(4)
+
+    def onehot(codes):
+        codes = jnp.broadcast_to(codes, (FRAMES, 8, FRAMES)).reshape(128, FRAMES)
+        diagonal = lax.broadcasted_iota(jnp.int32, (128, FRAMES), 0) // 8 == lanes((128, FRAMES))
+        codes = jnp.sum(jnp.where(diagonal, codes, 0), axis=1, keepdims=True)
+        return (codes == lanes((128, CODES))).astype(F32).astype(BF16)
+
+    def count_copy(k):
+        dest = (m + k) % NZ
+        return pltpu.make_async_remote_copy(
+            src_ref=count_send.at[dest], dst_ref=count_recv.at[k], send_sem=count_ss.at[k],
+            recv_sem=count_rs.at[k], device_id=(c, f, dest), device_id_type=MESH,
+        )
+
+    def all_count_copy(k):
+        return pltpu.make_async_remote_copy(
+            src_ref=count_all.at[f], dst_ref=count_all.at[f], send_sem=all_count_ss.at[k],
+            recv_sem=all_count_rs.at[k], device_id=frame_peer(k), device_id_type=MESH,
+        )
+
+    codes_copy.wait_recv()
+    hot[:128] = onehot(cidx_recv[...])
+    hot[128:] = onehot(cidx_ref[...])
+    counts = jnp.dot(jnp.ones((16, 256), BF16), hot[...], preferred_element_type=F32)
+    for dest in range(NZ):
+        count_send[dest] = counts[:, dest * 128 : dest * 128 + 128].astype(BF16)
+    for k in range(1, NZ):
+        count_copy(k).start()
+    count_recv[0] = count_send[m]
+    gather(GATHER_AT[4])
     for k in range(1, NZ):
         heads_copy(k).wait_recv()
 
@@ -312,7 +364,17 @@
         rows_copy(k).start()
 
     rows_recv[f] = rows_send[f]
-    gather(12)
+    for k in range(1, NZ):
+        count_copy(k).wait_recv()
+    counts = jnp.sum(count_recv[...].astype(F32), axis=0)
+    upper = jnp.floor(counts[:8] * (1.0 / 256.0))
+    count_all[f] = jnp.concatenate([counts[8:] - 256.0 * upper, upper], axis=0).astype(BF16)
+
+    @pl.loop(1, FRAMES)
+    def _(k):
+        all_count_copy(k).start()
+
+    gather(GATHER_AT[5])
 
     @pl.loop(1, FRAMES)
     def _(k):
@@ -320,156 +382,144 @@
 
     arrived = rows_recv[...].astype(F32)
     after_space = jnp.concatenate([arrived[:, :8], arrived[:, 8:]], axis=2).reshape(128, D)
-    for name in ("gt", "tp", "to", "gm", "cproj", "cidx"):
-        loads[name].wait()
     time_in = layer_norm(after_space, gt_ref[...].reshape(1, D)).astype(BF16)
     tq = jnp.dot(time_in, tp[0], preferred_element_type=F32) * (1.0 / math.sqrt(HD))
     tk = jnp.dot(time_in, tp[1], preferred_element_type=F32).astype(BF16)
     tv = jnp.dot(time_in, tp[2], preferred_element_type=F32).astype(BF16)
-    gather(1)
+    tq = tq.astype(BF16)
+    gather(GATHER_AT[6])
     row = lax.broadcasted_iota(jnp.int32, (128, 128), 0)
     col = lax.broadcasted_iota(jnp.int32, (128, 128), 1)
-    seen = (row % 8 == col % 8) & (col // 8 <= row // 8)
+    seen = ((row % 8 == col % 8) & (col // 8 <= row // 8))[None]
     low = col < HD
+    none = jnp.zeros((128, 128), BF16)
+    ones = jnp.ones((128, 128), BF16)
+    cuts = [slice(i * 128, i * 128 + 128) for i in range(T_HEADS // 2)]
+    scores = jnp.concatenate(
+        [
+            nt_dot(
+                jnp.concatenate(
+                    [jnp.where(low, tq[:, cut], none), jnp.where(low, none, tq[:, cut])], axis=0
+                ),
+                tk[:, cut],
+            )
+            for cut in cuts
+        ],
+        axis=0,
+    ).reshape(T_HEADS, 128, 128)
+    scores = jnp.where(seen, scores, -jnp.inf)
+    weights = jnp.exp(scores - jnp.max(scores, axis=-1, keepdims=True)).astype(BF16)
+    gather(GATHER_AT[7])
     pieces = []
-    for i in range(T_HEADS // 2):
-        cut = slice(i * 128, i * 128 + 128)
-        both = []
-        for own_half in (low, jnp.logical_not(low)):
-            scores = nt_dot(jnp.where(own_half, tq[:, cut], 0.0).astype(BF16), tk[:, cut])
-            scores = jnp.where(seen, scores, -jnp.inf)
-            weights = jnp.exp(scores - jnp.max(scores, axis=-1, keepdims=True))
-            weights = weights / jnp.sum(weights, axis=-1, keepdims=True)
-            both.append(jnp.dot(weights.astype(BF16), tv[:, cut], preferred_element_type=F32))
-        pieces.append(jnp.where(low, both[0], both[1]).astype(BF16))
-        gather((1, 2, 0, 2, 0, 2)[i])
+    for i, cut in enumerate(cuts):
+        both = jnp.dot(
+            weights[2 * i : 2 * i + 2].reshape(256, 128),
+            jnp.concatenate([tv[:, cut], ones], axis=1),
+            preferred_element_type=F32,
+        )
+        both = both[:, :128] / both[:, 128:]
+        pieces.append(jnp.where(low, both[:128], both[128:]).astype(BF16))
+    gather(GATHER_AT[8])
     time_heads = jnp.concatenate(pieces, axis=1)
     after_time = after_space + jnp.dot(time_heads, to[...], preferred_element_type=F32)
-    gather(2)
+    gather(GATHER_AT[9])
     act_send[...] = layer_norm(after_time, gm_ref[...].reshape(1, D)).astype(BF16)
 
-    partner = (1 - c, f, m)
-    act_copy = pltpu.make_async_remote_copy(
-        src_ref=act_send, dst_ref=act_recv, send_sem=pair_ss.at[0], recv_sem=pair_rs.at[0],
-        device_id=partner, device_id_type=MESH,
-    )
+    act_copy = pair_copy(0, act_send, act_recv)
     act_copy.start()
-    gather(7)
     act_copy.wait_recv()
     act = jnp.concatenate([act_recv[...], act_send[...]], axis=0)
     partial = jnp.zeros((256, D), F32)
-    for late in range(2):
-        for p in (1, 0, 2):
-            at3 = me[ORDERS[p][2]]
-            if p == 0:
-                steps = (6, 3, 5, 4) if late else (0, 1, 7, 2)
-            else:
-                steps = (3, 2) if late else (0, 1)
-            part = [gathered[p][(at3 + step) % SIZE[ORDERS[p][2]]] for step in steps]
-            w_in = jnp.concatenate([block[:, 0].reshape(-1, D) for block in part], axis=0)
-            w_out = jnp.concatenate([block[:, 1].reshape(-1, D) for block in part], axis=0)
-            hidden = gelu(nt_dot(act, w_in)).astype(BF16)
-            partial += jnp.dot(hidden, w_out, preferred_element_type=F32)
-        gather(len(todo))
+    for until, group_of in MLP_GROUPS:
+        gather(until)
+        w_in, w_out = [], []
+        for p, steps in group_of:
+            for step in steps:
+                block = gathered[p][(me[ORDERS[p][2]] + step) % SIZE[ORDERS[p][2]]]
+                w_in.append(block[:, 0].reshape(-1, D))
+                w_out.append(block[:, 1].reshape(-1, D))
+        hidden = gelu(nt_dot(act, jnp.concatenate(w_in, axis=0))).astype(BF16)
+        partial += jnp.dot(hidden, jnp.concatenate(w_out, axis=0), preferred_element_type=F32)
+
+    def red_copy(k):
+        return pltpu.make_async_remote_copy(
+            src_ref=red_send.at[(group + k) % 16], dst_ref=red_recv.at[k], send_sem=red_ss.at[k],
+            recv_sem=red_rs.at[k], device_id=group_peer(k), device_id_type=MESH,
+        )
+
+    after_time = after_time + partial[128:]
+    share = jnp.concatenate([partial[:128], after_time], axis=0).astype(BF16)
+    vecs = nt_dot(cproj_ref[...], share)
+    high = vecs.astype(BF16)
+    rest = (vecs - high.astype(F32)).astype(BF16)
+    sums = jnp.dot(
+        jnp.concatenate([high, rest], axis=0), hot[...], preferred_element_type=F32
+    )
+    sums = sums[:32] + sums[32:]
+    for dest in range(16):
+        low_row, low_lane = dest // NZ * 16, dest % NZ * 128
+        red_send[dest] = sums[low_row : low_row + 16, low_lane : low_lane + 128].astype(BF16)
+
+    @pl.loop(1, 16)
+    def _(k):
+        red_copy(k).start()
+
     back_send[...] = partial[:128]
-    back_copy = pltpu.make_async_remote_copy(
-        src_ref=back_send, dst_ref=back_recv, send_sem=pair_ss.at[1], recv_sem=pair_rs.at[1],
-        device_id=partner, device_id_type=MESH,
-    )
+    back_copy = pair_copy(1, back_send, back_recv)
     back_copy.start()
-    after_time = after_time + partial[128:]
-    codes = jnp.broadcast_to(cidx_ref[...], (FRAMES, 8, FRAMES)).reshape(128, FRAMES)
-    diagonal = lax.broadcasted_iota(jnp.int32, (128, FRAMES), 0) // 8 == lanes((128, FRAMES))
-    codes = jnp.sum(jnp.where(diagonal, codes, 0), axis=1, keepdims=True)
-    onehot = (codes == lanes((128, CODES))).astype(F32).astype(BF16)
+
+    def tot_copy(k):
+        return pltpu.make_async_remote_copy(
+            src_ref=tot_all.at[f], dst_ref=tot_all.at[f], send_sem=tot_ss.at[k],
+            recv_sem=tot_rs.at[k], device_id=frame_peer(k), device_id_type=MESH,
+        )
+
+    def mean_copy(k):
+        return pltpu.make_async_remote_copy(
+            src_ref=mean_send, dst_ref=mean_recv.at[group], send_sem=fin_ss.at[k],
+            recv_sem=fin_rs.at[k], device_id=group_peer(k), device_id_type=MESH,
+        )
+
+    gather_sent()
+    red_recv[0] = red_send[group]
+
+    @pl.loop(1, 16)
+    def _(k):
+        red_copy(k).wait_recv()
+
+    tot_all[f] = jnp.sum(red_recv[...].astype(F32), axis=0).astype(BF16)
+
+    @pl.loop(1, 16)
+    def _(k):
+        tot_copy(k).start()
+
     back_copy.wait_recv()
-    outputs = (after_time + back_recv[...]).astype(BF16)
-    out_s[0] = outputs.astype(F32).reshape(FRAMES, 8, D).astype(BF16)
+    outputs = (after_time + back_recv[...]).reshape(FRAMES, 8, D)
+    out_s[0] = outputs.astype(BF16)
     out_copy = pltpu.make_async_copy(out_s, out_hbm, load_sem.at[0])
     out_copy.start()
-
-    vecs = nt_dot(cproj_ref[...], outputs)
-    high = vecs.astype(BF16)
-    rest = (vecs - high.astype(F32)).astype(BF16)
-    left = jnp.concatenate([high, rest, jnp.ones((16, 128), BF16)], axis=0)
-    sums = jnp.dot(left, onehot, preferred_element_type=F32)
-    counts = sums[64:72]
-    sums = sums[:32] + sums[32:64]
-    for to_c in range(2):
-        for to_m in range(NZ):
-            cut = slice(to_m * 128, to_m * 128 + 128)
-            sums_send[to_c, to_m] = jnp.concatenate(
-                [sums[to_c * 16 : to_c * 16 + 16, cut], counts[:, cut]], axis=0
-            )
-    sums_copy = pltpu.make_async_remote_copy(
-        src_ref=sums_send.at[1 - c], dst_ref=sums_recv, send_sem=pair_ss.at[2],
-        recv_sem=pair_rs.at[2], device_id=partner, device_id_type=MESH,
-    )
-    sums_copy.start()
-
-    def coded(values):
-        many = values[..., 16:24, :]
-        upper = jnp.floor(many * (1.0 / 256.0))
-        return jnp.concatenate(
-            [values[..., :16, :], many - 256.0 * upper, upper], axis=-2
-        ).astype(BF16)
-
-    def decoded(values):
-        values = values.astype(F32)
-        return jnp.concatenate(
-            [values[..., :16, :], values[..., 16:24, :] + 256.0 * values[..., 24:, :]], axis=-2
-        )
-
-    def red_copy(k):
-        dest = (m + k) % NZ
-        return pltpu.make_async_remote_copy(
-            src_ref=red_send.at[dest], dst_ref=red_recv.at[k], send_sem=red_ss.at[k],
-            recv_sem=red_rs.at[k], device_id=(c, f, dest), device_id_type=MESH,
-        )
-
-    def tot_copy(k):
-        return pltpu.make_async_remote_copy(
-            src_ref=tot_all.at[f], dst_ref=tot_all.at[f], send_sem=tot_ss.at[k],
-            recv_sem=tot_rs.at[k], device_id=frame_peer(k), device_id_type=MESH,
-        )
-
-    def mean_copy(k):
-        return pltpu.make_async_remote_copy(
-            src_ref=mean_send, dst_ref=mean_recv.at[group], send_sem=fin_ss.at[k],
-            recv_sem=fin_rs.at[k], device_id=group_peer(k), device_id_type=MESH,
-        )
-
-    sums_copy.wait_recv()
-    red_send[...] = coded(sums_send[c] + sums_recv[...])
-    for k in (4, 3, 5, 2, 6, 1, 7):
-        red_copy(k).start()
-    gather_sent()
-    red_recv[0] = red_send[m]
-    for k in range(1, NZ):
-        red_copy(k).wait_recv()
-    tot_all[f] = coded(jnp.sum(decoded(red_recv[...]), axis=0))
-
-    @pl.loop(1, 16)
-    def _(k):
-        tot_copy(k).start()
-
     for k in range(1, NZ):
         heads_copy(k).wait_send()
+        count_copy(k).wait_send()
+    for copy in (codes_copy, act_copy, back_copy):
+        copy.wait_send()
+
+    @pl.loop(1, 16)
+    def _(k):
+        rows_copy(k).wait_send()
         red_copy(k).wait_send()
-    act_copy.wait_send()
-    back_copy.wait_send()
-    sums_copy.wait_send()
-
-    @pl.loop(1, 16)
-    def _(k):
-        rows_copy(k).wait_send()
+        all_count_copy(k).wait_send()
+        all_count_copy(k).wait_recv()
+
+    counts = jnp.sum(count_all[...].astype(F32), axis=0)
+    counts = jnp.maximum(counts[:8] + 256.0 * counts[8:], 1.0)
+    counts = jnp.concatenate([counts, counts], axis=0)
 
     @pl.loop(1, 16)
     def _(k):
         tot_copy(k).wait_recv()
 
-    total = jnp.sum(decoded(tot_all[...]), axis=0)
-    means = (total[:16] / jnp.maximum(total[16:17], 1.0)).astype(BF16)
+    means = (jnp.sum(tot_all[...].astype(F32), axis=0) / counts).astype(BF16)
     mean_send[...] = means
     mean_recv[group] = means
 
@@ -498,6 +548,7 @@
     args[2] = args[2].swapaxes(1, 2)
     args[10] = args[10].T
     args[11] = args[11].swapaxes(1, 2)
+    args = [pltpu.with_memory_space_constraint(arg, pltpu.HBM) for arg in args]
     vmem = pl.BlockSpec(memory_space=pltpu.VMEM)
     hbm = pl.BlockSpec(memory_space=pltpu.HBM)
     dma = pltpu.SemaphoreType.DMA
@@ -529,16 +580,19 @@
         for order, units in zip(ORDERS, UNITS)
     ]
     scratch += [
+        pltpu.VMEM((1, 8, FRAMES), jnp.int32),
+        pltpu.VMEM((256, CODES), BF16),
+        pltpu.VMEM((NZ, 16, 128), BF16),
+        pltpu.VMEM((NZ, 16, 128), BF16),
+        pltpu.VMEM((FRAMES, 16, 128), BF16),
         pltpu.VMEM((128, D), BF16),
         pltpu.VMEM((128, D), BF16),
         pltpu.VMEM((128, D), F32),
         pltpu.VMEM((128, D), F32),
         pltpu.VMEM((1, FRAMES, 8, D), BF16),
-        pltpu.VMEM((2, NZ, 24, 128), F32),
-        pltpu.VMEM((NZ, 24, 128), F32),
-        pltpu.VMEM((NZ, 32, 128), BF16),
-        pltpu.VMEM((NZ, 32, 128), BF16),
-        pltpu.VMEM((FRAMES, 32, 128), BF16),
+        pltpu.VMEM((16, 16, 128), BF16),
+        pltpu.VMEM((16, 16, 128), BF16),
+        pltpu.VMEM((FRAMES, 16, 128), BF16),
         pltpu.VMEM((16, 128), BF16),
         pltpu.VMEM((16, 16, 128), BF16),
     ]
@@ -550,8 +604,10 @@
         dma((3, 4)), dma((3, 4)),
         dma((3, 4, 4, 2)), dma((3, 4, 4, 2)),
         dma((3,)), dma((3,)),
+        dma((16,)), dma((16,)),
+        dma((16,)), dma((16,)),
+        dma((16,)), dma((16,)),
         dma((NZ,)), dma((NZ,)),
-        dma((16,)), dma((16,)),
         dma((16,)), dma((16,)),
     ]
     block_out, means = pl.pallas_call(
@@ -564,7 +620,7 @@
         out_specs=(hbm, vmem),
         scratch_shapes=scratch,
         compiler_params=pltpu.CompilerParams(
-            collective_id=0, has_side_effects=True, vmem_limit_bytes=60 * 1024 * 1024
+            collective_id=0, has_side_effects=True, vmem_limit_bytes=52 * 1024 * 1024
         ),
     )(*args)
     return block_out, means.T

time: 69 us -> 62.5 us (0.906)
  Pallas kernels: 65.1 us -> 60.4 us
  local copies, waits for them, and re-layouts: 3.18 us -> 1.33 us
    pallas_call x1, Pallas kernels: 65.1 us -> 60.4 us  [shards(): pl.pallas_call(block_kernel, out_shape=(jax.ShapeDtypeStruct((1, FRAMES,...]
    unnamed x2, local copies, waits for them, and re-layouts: 3.18 us -> 1.33 us
where the time goes in v3:
time: 62.5 us; the launch traced here: 62.4 us
  Pallas kernels  60.4 us (97%)
  local copies, waits for them, and re-layouts  1.33 us (2%)
  between operations  0.64 us (1%)
    pallas_call x1, Pallas kernels, shards(): pl.pallas_call(block_kernel, out_shape=(jax.ShapeDtypeStruct((1, FRAMES,...  60.4 us
    unnamed x2, local copies, waits for them, and re-layouts  1.33 us

profile of v3, /device:TPU:1, one launch (start us, length us, event | category | flops | bytes accessed | tf_op | source)
XLA Modules:
  0.0 62.4 jit_solution(17288019278705364340)
XLA Ops:
  0.6 60.4 %shard_map.131 = (bf16[1,16,8,768]{3,2,1,0:T(8,128)(2,1)S(1)}, f32[32,1024]{1,0:T(8,128)S(1)}) custom-call(bf16[1,1,1024,768]{3,2,1,0:T(8,128)(2,1)} %frames_hbm.1, f32[768]{0:T(1024)} %gs_hbm.1, bf16[3,64,768]{2,1,0:T(8,128)(2,1)} %bitcast.5, bf16[512,768]{1,0:T(8,128)(2,1)} %sout_hbm.1, f32[768]{0:T(1024)} %gt_hbm.1, bf16[3,768,768]{2,1,0:T(8,128)(2,1)} %tproj_hbm.1, ...), custom_call_target="tpu_custom_call" | custom-call | tf_op jit(solution)/shard_map/pallas_call | solution.py:613
  61.0 0.7 %copy.16 = bf16[1,16,8,768]{3,2,1,0:T(8,128)(2,1)} copy(bf16[1,16,8,768]{3,2,1,0:T(8,128)(2,1)S(1)} %get-tuple-element.8) | data formatting | bytes 393216
  61.7 0.7 %copy.17 = f32[1024,32]{0,1:T(8,128)} copy(f32[1024,32]{0,1:T(8,128)S(1)} %bitcast.4) | data formatting | bytes 262144

commit v4 on v3

--- a/solution.py
+++ b/solution.py
@@ -34,7 +34,7 @@
     (2, 2, 2, 0), (0, 2, 4, 0), (0, 2, 4, 1), (1, 2, 2, 1), (2, 2, 2, 1),
     (0, 2, 4, 3), (1, 2, 2, 3), (0, 2, 4, 2), (2, 2, 2, 3), (1, 2, 2, 2), (2, 2, 2, 2),
 )
-GATHER_AT = (0, 0, 0, 1, 6, 21, 22, 26, 28, 29)
+GATHER_AT = (0, 1, 1, 1, 6, 23, 24, 27, 28, 29)
 MLP_GROUPS = (
     (29, ((0, (0, 1, 7, 2)),)),
     (32, ((2, (0, 1)),)),
@@ -233,6 +233,21 @@
                     for way in range(2):
                         ring_copy(p, step, sub, way).wait_send()
 
+    partner = (1 - c, f, m)
+
+    def pair_copy(i, src, dst):
+        return pltpu.make_async_remote_copy(
+            src_ref=src, dst_ref=dst, send_sem=pair_ss.at[i], recv_sem=pair_rs.at[i],
+            device_id=partner, device_id_type=MESH,
+        )
+
+    loads["cidx"].wait()
+    pl.semaphore_wait(barrier, 30)
+    for p in range(3):
+        first_send(p)
+    codes_copy = pair_copy(2, cidx_ref, cidx_recv)
+    codes_copy.start()
+
     for name in ("gs", "sp", "fr"):
         loads[name].wait()
     wqkv = jnp.concatenate([sp[...].reshape(3 * HD, D), jnp.zeros((HD, D), BF16)], axis=0)
@@ -253,22 +268,6 @@
             q_s[to_m, pl.ds(pl.multiple_of(i * 32, 32), 32), :] = (
                 q[:, to_m].reshape(32, 128).astype(BF16)
             )
-
-    partner = (1 - c, f, m)
-
-    def pair_copy(i, src, dst):
-        return pltpu.make_async_remote_copy(
-            src_ref=src, dst_ref=dst, send_sem=pair_ss.at[i], recv_sem=pair_rs.at[i],
-            device_id=partner, device_id_type=MESH,
-        )
-
-    for name in ("gt", "tp", "to", "gm", "cproj", "cidx"):
-        loads[name].wait()
-    pl.semaphore_wait(barrier, 30)
-    for p in range(3):
-        first_send(p)
-    codes_copy = pair_copy(2, cidx_ref, cidx_recv)
-    codes_copy.start()
 
     def heads_copy(shift):
         dest = (m + shift) % NZ
@@ -380,6 +379,8 @@
     def _(k):
         rows_copy(k).wait_recv()
 
+    for name in ("gt", "tp", "to", "gm", "cproj"):
+        loads[name].wait()
     arrived = rows_recv[...].astype(F32)
     after_space = jnp.concatenate([arrived[:, :8], arrived[:, 8:]], axis=2).reshape(128, D)
     time_in = layer_norm(after_space, gt_ref[...].reshape(1, D)).astype(BF16)

time: 62.5 us -> 61.3 us (0.981)
  Pallas kernels: 60.4 us -> 59.3 us
    pallas_call x1, Pallas kernels: 60.4 us -> 59.3 us  [shards(): pl.pallas_call(block_kernel, out_shape=(jax.ShapeDtypeStruct((1, FRAMES,...]
where the time goes in v4:
time: 61.3 us
  Pallas kernels  59.3 us (97%)
  local copies, waits for them, and re-layouts  1.33 us (2%)
  between operations  0.64 us (1%)
    pallas_call x1, Pallas kernels, shards(): pl.pallas_call(block_kernel, out_shape=(jax.ShapeDtypeStruct((1, FRAMES,...  59.3 us
    unnamed x2, local copies, waits for them, and re-layouts  1.33 us

profile of v4, /device:TPU:1, one launch (start us, length us, event | category | flops | bytes accessed | tf_op | source)
XLA Modules:
  0.0 61.3 jit_solution(5347544627681081139)
XLA Ops:
  0.6 59.3 %shard_map.131 = (bf16[1,16,8,768]{3,2,1,0:T(8,128)(2,1)S(1)}, f32[32,1024]{1,0:T(8,128)S(1)}) custom-call(bf16[1,1,1024,768]{3,2,1,0:T(8,128)(2,1)} %frames_hbm.1, f32[768]{0:T(1024)} %gs_hbm.1, bf16[3,64,768]{2,1,0:T(8,128)(2,1)} %bitcast.5, bf16[512,768]{1,0:T(8,128)(2,1)} %sout_hbm.1, f32[768]{0:T(1024)} %gt_hbm.1, bf16[3,768,768]{2,1,0:T(8,128)(2,1)} %tproj_hbm.1, ...), custom_call_target="tpu_custom_call" | custom-call | tf_op jit(solution)/shard_map/pallas_call | solution.py:614
  59.9 0.7 %copy.16 = bf16[1,16,8,768]{3,2,1,0:T(8,128)(2,1)} copy(bf16[1,16,8,768]{3,2,1,0:T(8,128)(2,1)S(1)} %get-tuple-element.8) | data formatting | bytes 393216
  60.6 0.7 %copy.17 = f32[1024,32]{0,1:T(8,128)} copy(f32[1024,32]{0,1:T(8,128)S(1)} %bitcast.4) | data formatting | bytes 262144

commit v5 on v4

--- a/solution.py
+++ b/solution.py
@@ -43,6 +43,8 @@
     (41, ((2, (3,)), (0, (4,)))),
     (44, ((1, (2,)), (2, (2,)))),
 )
+FRAME_ORDER = sorted(range(1, 16), key=lambda k: -min(k // 4, 4 - k // 4) - min(k % 4, 4 - k % 4))
+GROUP_ORDER = sorted(range(1, 16), key=lambda k: -min(k % 8, 8 - k % 8))
 SOURCES = {"x": ((0, 1), (2, 3)), "z": ((0, 1), (2, 7), (6, 3), (4, 5))}
 
 
@@ -93,18 +95,17 @@
         return (c, x * NY + y, moved.get("z", m))
 
     def frame_peer(k):
-        return (c, (f + k) % FRAMES, m)
+        return at(x=(me["x"] + k // NY) % NX, y=(me["y"] + k % NY) % NY)
 
     def group_peer(k):
-        other = (group + k) % 16
-        return (other // NZ, f, other % NZ)
+        return ((c + k // NZ) % 2, f, (m + k % NZ) % NZ)
 
     barrier = pltpu.get_barrier_semaphore()
 
-    @pl.loop(1, 16)
-    def _(k):
+    for k in GROUP_ORDER:
+        pl.semaphore_signal(barrier, inc=1, device_id=group_peer(k), device_id_type=MESH)
+    for k in FRAME_ORDER:
         pl.semaphore_signal(barrier, inc=1, device_id=frame_peer(k), device_id_type=MESH)
-        pl.semaphore_signal(barrier, inc=1, device_id=group_peer(k), device_id_type=MESH)
 
     loads = {}
     for name, src, dst in (
@@ -351,15 +352,14 @@
     rows_send[...] = jnp.concatenate([split[:, :, :HALF], split[:, :, HALF:]], axis=1).astype(BF16)
 
     def rows_copy(k):
-        dest = (f + k) % FRAMES
-        return pltpu.make_async_remote_copy(
-            src_ref=rows_send.at[dest], dst_ref=rows_recv.at[f],
+        peer = frame_peer(k)
+        return pltpu.make_async_remote_copy(
+            src_ref=rows_send.at[peer[1]], dst_ref=rows_recv.at[f],
             send_sem=rows_ss.at[k], recv_sem=rows_rs.at[k],
-            device_id=(c, dest, m), device_id_type=MESH,
-        )
-
-    @pl.loop(1, FRAMES)
-    def _(k):
+            device_id=peer, device_id_type=MESH,
+        )
+
+    for k in FRAME_ORDER:
         rows_copy(k).start()
 
     rows_recv[f] = rows_send[f]
@@ -369,8 +369,7 @@
     upper = jnp.floor(counts[:8] * (1.0 / 256.0))
     count_all[f] = jnp.concatenate([counts[8:] - 256.0 * upper, upper], axis=0).astype(BF16)
 
-    @pl.loop(1, FRAMES)
-    def _(k):
+    for k in FRAME_ORDER:
         all_count_copy(k).start()
 
     gather(GATHER_AT[5])
@@ -443,9 +442,10 @@
         partial += jnp.dot(hidden, jnp.concatenate(w_out, axis=0), preferred_element_type=F32)
 
     def red_copy(k):
-        return pltpu.make_async_remote_copy(
-            src_ref=red_send.at[(group + k) % 16], dst_ref=red_recv.at[k], send_sem=red_ss.at[k],
-            recv_sem=red_rs.at[k], device_id=group_peer(k), device_id_type=MESH,
+        peer = group_peer(k)
+        return pltpu.make_async_remote_copy(
+            src_ref=red_send.at[peer[0] * NZ + peer[2]], dst_ref=red_recv.at[k],
+            send_sem=red_ss.at[k], recv_sem=red_rs.at[k], device_id=peer, device_id_type=MESH,
         )
 
     after_time = after_time + partial[128:]
@@ -461,8 +461,7 @@
         low_row, low_lane = dest // NZ * 16, dest % NZ * 128
         red_send[dest] = sums[low_row : low_row + 16, low_lane : low_lane + 128].astype(BF16)
 
-    @pl.loop(1, 16)
-    def _(k):
+    for k in GROUP_ORDER:
         red_copy(k).start()
 
     back_send[...] = partial[:128]
@@ -490,8 +489,7 @@
 
     tot_all[f] = jnp.sum(red_recv[...].astype(F32), axis=0).astype(BF16)
 
-    @pl.loop(1, 16)
-    def _(k):
+    for k in FRAME_ORDER:
         tot_copy(k).start()
 
     back_copy.wait_recv()
@@ -524,8 +522,7 @@
     mean_send[...] = means
     mean_recv[group] = means
 
-    @pl.loop(1, 16)
-    def _(k):
+    for k in GROUP_ORDER:
         mean_copy(k).start()
 
     @pl.loop(1, 16)

time: 61.3 us -> 61.2 us (level)
  no operation moved by 1% of the time
where the time goes in v5:
time: 61.2 us
  Pallas kernels  59.2 us (97%)
  local copies, waits for them, and re-layouts  1.33 us (2%)
  between operations  0.64 us (1%)
    pallas_call x1, Pallas kernels, shards(): pl.pallas_call(block_kernel, out_shape=(jax.ShapeDtypeStruct((1, FRAMES,...  59.2 us
    unnamed x2, local copies, waits for them, and re-layouts  1.33 us

profile of v5, /device:TPU:1, one launch (start us, length us, event | category | flops | bytes accessed | tf_op | source)
XLA Modules:
  0.0 61.2 jit_solution(16530133571157087882)
XLA Ops:
  0.6 59.2 %shard_map.131 = (bf16[1,16,8,768]{3,2,1,0:T(8,128)(2,1)S(1)}, f32[32,1024]{1,0:T(8,128)S(1)}) custom-call(bf16[1,1,1024,768]{3,2,1,0:T(8,128)(2,1)} %frames_hbm.1, f32[768]{0:T(1024)} %gs_hbm.1, bf16[3,64,768]{2,1,0:T(8,128)(2,1)} %bitcast.5, bf16[512,768]{1,0:T(8,128)(2,1)} %sout_hbm.1, f32[768]{0:T(1024)} %gt_hbm.1, bf16[3,768,768]{2,1,0:T(8,128)(2,1)} %tproj_hbm.1, ...), custom_call_target="tpu_custom_call" | custom-call | tf_op jit(solution)/shard_map/pallas_call | solution.py:611
  59.8 0.7 %copy.16 = bf16[1,16,8,768]{3,2,1,0:T(8,128)(2,1)} copy(bf16[1,16,8,768]{3,2,1,0:T(8,128)(2,1)S(1)} %get-tuple-element.8) | data formatting | bytes 393216
  60.5 0.7 %copy.17 = f32[1024,32]{0,1:T(8,128)} copy(f32[1024,32]{0,1:T(8,128)S(1)} %bitcast.4) | data formatting | bytes 262144

commit v6 on v5

--- a/solution.py
+++ b/solution.py
@@ -374,8 +374,7 @@
 
     gather(GATHER_AT[5])
 
-    @pl.loop(1, FRAMES)
-    def _(k):
+    for k in reversed(FRAME_ORDER):
         rows_copy(k).wait_recv()
 
     for name in ("gt", "tp", "to", "gm", "cproj"):
@@ -483,8 +482,7 @@
     gather_sent()
     red_recv[0] = red_send[group]
 
-    @pl.loop(1, 16)
-    def _(k):
+    for k in reversed(GROUP_ORDER):
         red_copy(k).wait_recv()
 
     tot_all[f] = jnp.sum(red_recv[...].astype(F32), axis=0).astype(BF16)
@@ -514,8 +512,7 @@
     counts = jnp.maximum(counts[:8] + 256.0 * counts[8:], 1.0)
     counts = jnp.concatenate([counts, counts], axis=0)
 
-    @pl.loop(1, 16)
-    def _(k):
+    for k in reversed(FRAME_ORDER):
         tot_copy(k).wait_recv()
 
     means = (jnp.sum(tot_all[...].astype(F32), axis=0) / counts).astype(BF16)
@@ -532,8 +529,7 @@
 
     out_copy.wait()
 
-    @pl.loop(1, 16)
-    def _(k):
+    for k in reversed(GROUP_ORDER):
         mean_copy(k).wait_recv()
 
     for g in range(16):

time: 61.2 us -> 61.2 us (level)
  no operation moved by 1% of the time
where the time goes in v6:
time: 61.2 us; the launch traced here: 61.1 us
  Pallas kernels  59.2 us (97%)
  local copies, waits for them, and re-layouts  1.33 us (2%)
  between operations  0.64 us (1%)
    pallas_call x1, Pallas kernels, shards(): pl.pallas_call(block_kernel, out_shape=(jax.ShapeDtypeStruct((1, FRAMES,...  59.2 us
    unnamed x2, local copies, waits for them, and re-layouts  1.33 us

profile of v6, /device:TPU:1, one launch (start us, length us, event | category | flops | bytes accessed | tf_op | source)
XLA Modules:
  0.0 61.1 jit_solution(10028356148983487051)
XLA Ops:
  0.6 59.2 %shard_map.131 = (bf16[1,16,8,768]{3,2,1,0:T(8,128)(2,1)S(1)}, f32[32,1024]{1,0:T(8,128)S(1)}) custom-call(bf16[1,1,1024,768]{3,2,1,0:T(8,128)(2,1)} %frames_hbm.1, f32[768]{0:T(1024)} %gs_hbm.1, bf16[3,64,768]{2,1,0:T(8,128)(2,1)} %bitcast.5, bf16[512,768]{1,0:T(8,128)(2,1)} %sout_hbm.1, f32[768]{0:T(1024)} %gt_hbm.1, bf16[3,768,768]{2,1,0:T(8,128)(2,1)} %tproj_hbm.1, ...), custom_call_target="tpu_custom_call" | custom-call | tf_op jit(solution)/shard_map/pallas_call | solution.py:607
  59.8 0.7 %copy.16 = bf16[1,16,8,768]{3,2,1,0:T(8,128)(2,1)} copy(bf16[1,16,8,768]{3,2,1,0:T(8,128)(2,1)S(1)} %get-tuple-element.8) | data formatting | bytes 393216
  60.5 0.7 %copy.17 = f32[1024,32]{0,1:T(8,128)} copy(f32[1024,32]{0,1:T(8,128)S(1)} %bitcast.4) | data formatting | bytes 262144
